TPU v7x, 256 devices: a whole 4x4x8 slice. The times are simulated.
256 devices in a mesh: tm: 64 (over y, z, core), space: 4 (over x).
Axes of the slice: x: 4, y: 4, z: 8, core: 2. Of those that a mesh axis runs over, the one named last changes fastest.
Arguments:
- frames: bfloat16 [256, 32, 24, 384], P('tm', 'space'), may hold values from -6 to 6
- conv_weight: bfloat16 [27, 384, 384], replicated, may hold values from -0.0625 to 0.0625
- head_weight: bfloat16 [384, 32], replicated, may hold values from -0.3125 to 0.3125
- clip_len: int32 [21], replicated, may hold values from 1 to 21, 256 in all
Outputs:
- latent: float32 [256, 32, 24, 32], P('tm', 'space')
- loss: float32 [], replicated
- weight_grad: float32 [27, 384, 384], P(None, 'tm', 'space')
- head_grad: float32 [384, 32], P('tm', 'space')
Inputs may be any that keep to these rules, and one draw needn't show every extreme that they name: `clip_len`: the lengths sum to 256; the longest clip has exactly 21 frames.
All inputs are finite; a program needn't handle non-finite values.
Results may differ from a plain program's by a relative error of at most 0.003.
Values may be sent and summed in bfloat16 or wider, within the bound.
No kernel may reach another device: no remote copies, remote signals or barrier semaphores. Data moves between devices by JAX's collectives and lax.ppermute only.
A program may use at most 256 MiB of HBM per device.

v0:
```python
import jax
import jax.numpy as jnp
from jax import lax
from jax.sharding import PartitionSpec as P


def passed_along(value, axis, steps):
    count = lax.axis_size(axis)
    initial, last = (max(0, -steps), min(count, count - steps))
    return lax.ppermute(value, axis, [(source, source + steps) for source in range(initial, last)])


def padded(cells, sides, width):
    for axis, dim in sides:
        count = lax.axis_size(axis)
        ends = count - 1
        head = lax.slice_in_dim(cells, 0, width, axis=dim)
        tail = lax.slice_in_dim(cells, cells.shape[dim] - width, cells.shape[dim], axis=dim)
        cells = jnp.concatenate(
            [
                lax.ppermute(tail, axis, [(i, (i + 1) % count) for i in range(ends)]),
                cells,
                lax.ppermute(head, axis, [((i + 1) % count, i) for i in range(ends)]),
            ],
            axis=dim,
        )
    return cells


def tap_patches(extended, pos, nframe, nrow, ncol):
    chans = extended.shape[-1]
    cells = nframe * nrow * ncol
    widened = jnp.pad(extended, ((0, 0), (0, 0), (1, 1), (0, 0)))
    pieces = []
    for tap in range(27):
        dt, dh, dw = (tap // 9, tap // 3 % 3, tap % 3)
        piece = widened[dt : dt + nframe, dh : dh + nrow, dw : dw + ncol, :]
        keep = (pos >= 2 - dt).astype(extended.dtype)
        pieces.append((piece * keep[:, None, None, None]).reshape(cells, chans))
    return jnp.concatenate(pieces, axis=1)


def body(frames, conv_weight, head_weight, clip_len):
    nframe, nrow, ncol, chans = frames.shape
    n_space = lax.axis_size("space")
    slab = lax.axis_index("tm")
    ends = jnp.cumsum(clip_len)
    starts = ends - clip_len
    frame_ids = slab * nframe + jnp.arange(nframe, dtype=jnp.int32)
    member = (frame_ids[:, None] >= starts[None, :]) & (frame_ids[:, None] < ends[None, :])
    pos = frame_ids - jnp.sum(member.astype(jnp.int32) * starts[None, :], axis=1)
    member = member.astype(jnp.float32)
    past = passed_along(frames[nframe - 2 :], "tm", 1)
    extended = jnp.concatenate([past, frames], axis=0)
    extended = padded(extended, (("space", 1),), 1)
    patches = tap_patches(extended, pos, nframe, nrow, ncol)
    pre = jnp.dot(
        patches, conv_weight.reshape(27 * chans, chans), preferred_element_type=jnp.float32
    )
    act = jax.nn.silu(pre).astype(jnp.bfloat16)
    latent = jnp.dot(act, head_weight, preferred_element_type=jnp.float32)
    zdim = latent.shape[1] // 2
    mean, logvar = (latent[:, :zdim], latent[:, zdim:])
    kcell = 0.5 * jnp.sum(mean * mean + jnp.exp(logvar) - 1.0 - logvar, axis=1)
    kframe = jnp.sum(kcell.reshape(nframe, nrow * ncol), axis=1)
    partial_sums = jnp.sum(member * kframe[:, None], axis=0)
    totals = lax.psum(partial_sums, ("tm", "space"))
    lens = clip_len.astype(jnp.float32)
    per_frame = float(nrow * n_space * ncol)
    loss = jnp.sum(lens * jnp.log1p(totals / (lens * per_frame)))
    gclip = lens / (lens * per_frame + totals)
    gframe = jnp.sum(member * gclip[None, :], axis=1)
    gcell = jnp.repeat(gframe, nrow * ncol)[:, None]
    dlat = jnp.concatenate([gcell * mean, gcell * 0.5 * (jnp.exp(logvar) - 1.0)], axis=1).astype(
        jnp.bfloat16
    )
    dact = lax.dot_general(
        dlat, head_weight, (((1,), (1,)), ((), ())), preferred_element_type=jnp.float32
    )
    sig = jax.nn.sigmoid(pre)
    dpre = (dact * sig * (1.0 + pre * (1.0 - sig))).astype(jnp.bfloat16)
    head_part = lax.dot_general(
        act, dlat, (((0,), (0,)), ((), ())), preferred_element_type=jnp.float32
    )
    weight_part = lax.dot_general(
        patches, dpre, (((0,), (0,)), ((), ())), preferred_element_type=jnp.float32
    )
    weight_part = weight_part.reshape(27, chans, chans)
    weight_half, head_half = (
        lax.psum_scatter(weight_part, "space", scatter_dimension=2, tiled=True),
        lax.psum_scatter(head_part, "space", scatter_dimension=1, tiled=True),
    )
    weight_grad, head_grad = (
        lax.psum_scatter(weight_half, "tm", scatter_dimension=1, tiled=True),
        lax.psum_scatter(head_half, "tm", scatter_dimension=0, tiled=True),
    )
    return (latent.reshape(nframe, nrow, ncol, 2 * zdim), loss, weight_grad, head_grad)


def solution(mesh):
    in_specs = (P("tm", "space", None, None), P(), P(), P())
    out_specs = (P("tm", "space", None, None), P(), P(None, "tm", "space"), P("tm", "space"))
    return jax.shard_map(body, mesh=mesh, in_specs=in_specs, out_specs=out_specs, check_vma=False)
```

profile of v0, /device:TPU:32, one launch (start us, length us, event | category | flops | bytes accessed | tf_op | source)
XLA Modules:
  0.0 609.2 jit_solution(8230170114786356119)
XLA Ops:
  7.2 1.0 slice.112
  8.2 1.9 collective-permute-start
  10.2 0.7 copy.26
  10.9 0.1 reduce
  11.1 0.7 sub.28
  11.7 0.2 select_reduce_fusion.2
  11.9 4.3 collective-permute-done
  16.3 1.7 broadcast_multiply_fusion
  18.0 3.4 collective-permute-start.1
  21.4 1.3 collective-permute-start.2
  22.7 1.0 collective-permute-done.1
  23.7 4.3 collective-permute-done.2
  28.0 0.8 fusion.5
  28.8 0.7 slice_multiply_fusion.13
  29.6 1.9 slice_multiply_fusion
  31.4 0.8 fusion.21
  35.0 19.3 %multiply_convert_fusion = (bf16[768,384]{1,0:T(8,128)(2,1)S(1)}, f32[768,384]{1,0:T(8,128)S(1)}) fusion(bf16[768,10368]{1,0:T(8,128)(2,1)S(1)} %constant_dynamic-update-slice_fusion.2, bf16[10368,384]{1,0:T(8,128)(2,1)} %bitcast.72), kind=kOutput, calls=%fused_computation.19 | convolution fusion | flops 6116769792 | bytes 25657344 | tf_op jit(solution)/shard_map/dot_general | solution.py:57
  54.3 0.3 fusion.31
  54.7 0.1 reduce_sum.56
  55.0 78.1 %psum.7 = f32[21]{0:T(128)S(1)} all-reduce(f32[21]{0:T(128)S(1)} %select_reduce_fusion.1), channel_id=1, replica_groups=mesh['tm'=64,'space'=4] {'tm','space'}, use_global_device_ids=true, to_apply=%region_5.6 | all-reduce | flops 21 | bytes 168 | tf_op jit(solution)/shard_map/psum | solution.py:67
  133.0 0.6 add_divide_fusion.2
  133.9 16.0 %fusion.8 = f32[10368,384]{1,0:T(8,128)} fusion(bf16[768,10368]{1,0:T(8,128)(2,1)} %copy-done.1, bf16[384,32]{0,1:T(8,128)(2,1)S(1)} %copy-done, f32[768,384]{1,0:T(8,128)S(1)} %get-tuple-element.73, bf16[768,16]{0,1:T(8,128)(2,1)S(1)} %get-tuple-element.66, bf16[768,16]{0,1:T(8,128)(2,1)S(1)} %get-tuple-element.65), kind=kOutput, calls=%fused_computation.11 | convolution fusion | flops 6136922112 | bytes 33103872 | tf_op jit(solution)/shard_map/dot_general | solution.py:85
  150.0 19.0 %copy.27 = f32[27,384,384]{1,0,2:T(8,128)} copy(f32[27,384,384]{2,1,0:T(8,128)} %bitcast.42) | data formatting | bytes 31850496 | tf_op jit(solution)/shard_map/reshape | solution.py:88
  169.1 164.1 %reduce-scatter.4.cloned.1.call-done = f32[27,384,96]{1,0,2:T(8,128)} async-done(((f32[27,384,384]{1,0,2:T(8,128)}), f32[27,384,96]{1,0,2:T(8,128)}) %reduce-scatter.4.cloned.1.call-update) | async-done | bytes 3981328 | tf_op jit(solution)/shard_map/reduce_scatter | solution.py:90
  333.2 6.3 %copy.28 = f32[27,384,96]{2,0,1:T(8,128)} copy(f32[27,384,96]{1,0,2:T(8,128)} %reduce-scatter.4.cloned.1.call-done) | data formatting | bytes 7962624 | tf_op jit(solution)/shard_map/reduce_scatter | solution.py:90
  339.5 0.6 dynamic-slice
  340.1 0.6 dynamic-slice.2
  342.0 0.9 copy.31
  342.9 0.2 fusion.23
  343.1 15.6 %all-reduce.1 = f32[384,32]{0,1:T(8,128)S(1)} all-reduce(f32[384,32]{0,1:T(8,128)S(1)} %fusion.23), channel_id=4, replica_groups=mesh['tm'=64,'space'=4] {'space'}, use_global_device_ids=true, to_apply=%region_10.11.clone | all-reduce | flops 12288 | bytes 98304
  358.7 242.9 %all-reduce.2 = f32[384,8]{0,1:T(8,128)S(1)} all-reduce(f32[384,8]{0,1:T(8,128)S(1)} %constant_dynamic-slice_fusion.1), channel_id=5, replica_groups=mesh['tm'=64,'space'=4] {'tm'}, use_global_device_ids=true, to_apply=%region_11.12.clone | all-reduce | flops 3072 | bytes 24576
  601.7 0.7 copy.30
  (58 shorter events, 3.4 us)
Async XLA Ops:
  7.2 47.2 %copy-start = (bf16[384,32]{0,1:T(8,128)(2,1)S(1)}, bf16[384,32]{0,1:T(8,128)(2,1)}, u32[]{:S(2)}) copy-start(bf16[384,32]{0,1:T(8,128)(2,1)} %param.6) | copy-start | bytes 73732
  7.2 326.0 %reduce-scatter.4.cloned.1.call-start = ((), (), s32[]{:S(2)}) async-start(), calls=%async_computation.2 | async-start | bytes 23592960 | tf_op jit(solution)/shard_map/reduce_scatter | solution.py:90
  8.2 8.0 %collective-permute-start = (bf16[2,8,24,384]{3,2,1,0:T(8,128)(2,1)S(1)}, bf16[2,8,24,384]{3,2,1,0:T(8,128)(2,1)S(1)}, u32[]{:S(2)}, u32[]{:S(2)}) collective-permute-start(bf16[2,8,24,384]{3,2,1,0:T(8,128)(2,1)S(1)} %slice.112), channel_id=1, source_target_pairs={{0,4},{4,8},{8,12},{12,16},{16,20},{20,24},{24,28},{28,32},{32,36}... | collective-permute-start | bytes 884744 | tf_op jit(solution)/shard_map/ppermute | solution.py:10
  18.0 5.7 collective-permute-start.1
  21.4 6.6 %collective-permute-start.2 = (bf16[6,1,24,384]{3,2,1,0:T(8,128)(2,1)S(1)}, bf16[6,1,24,384]{3,2,1,0:T(8,128)(2,1)S(1)}, u32[]{:S(2)}, u32[]{:S(2)}) collective-permute-start(bf16[6,1,24,384]{3,2,1,0:T(8,128)(2,1)S(1)} %get-tuple-element.62), channel_id=1, source_target_pairs={{1,0},{2,1},{3,2},{5,4},{6,5},{7,6},{9,8},{10,9},{11,10},{13,12},{... | collective-permute-start | bytes 331784 | tf_op jit(solution)/shard_map/ppermute | solution.py:23
  35.0 19.3 %copy-start.1 = (bf16[768,10368]{1,0:T(8,128)(2,1)}, bf16[768,10368]{1,0:T(8,128)(2,1)S(1)}, u32[]{:S(2)}) copy-start(bf16[768,10368]{1,0:T(8,128)(2,1)S(1)} %constant_dynamic-update-slice_fusion.2) | copy-start | bytes 47775748
  35.0 98.0 %copy-start.2 = (s32[21]{0:T(128)S(1)}, s32[21]{0:T(128)}, u32[]{:S(2)}) copy-start(s32[21]{0:T(128)} %param.7) | copy-start | bytes 256
  169.0 170.5 %copy-start.4 = (u32[256]{0:T(256)S(1)}, u32[256]{0:T(256)}, u32[]{:S(2)}) copy-start(u32[256]{0:T(256)} %constant.43) | copy-start | bytes 3076
  169.0 171.1 %copy-start.3 = (u32[256]{0:T(256)S(1)}, u32[256]{0:T(256)}, u32[]{:S(2)}) copy-start(u32[256]{0:T(256)} %constant.47) | copy-start | bytes 3076
  169.0 433.3 %reduce-scatter.6.cloned.1.call-start = ((), (), s32[]{:S(2)}) async-start(), calls=%async_computation.3 | async-start | bytes 6389760 | tf_op jit(solution)/shard_map/reduce_scatter | solution.py:94
Sparse Core Ops, SparseCore 0:
  169.2 164.0 reduce-scatter.3
  339.6 146.8 reduce-scatter.5
where the time goes:
time: 614 us; the launch traced here: 609 us
  blocking collectives  337 us (55%)
  waiting for transfers between devices  174 us (28%)
  matrix products  35.8 us (6%)
  local copies, waits for them, and re-layouts  32.7 us (5%)
  between operations  15.7 us (3%)
  other arithmetic  7.83 us (1%)
  starting transfers between devices  6.69 us (1%)
    unnamed x2, blocking collectives  258 us
    reduce_scatter x1, waiting for transfers between devices, body(): lax.psum_scatter(weight_part, 'space', scatter_dimension=2, tiled=True)  164 us
    psum x1, blocking collectives, body(): totals = lax.psum(partial_sums, ('tm', 'space'))  78.1 us
    dot_general x1, matrix products, body(): jnp.dot(patches, conv_weight.reshape(27 * chans, chans), preferred_elemen...  19.3 us
    reshape x1, local copies, waits for them, and re-layouts, body(): weight_part = weight_part.reshape(27, chans, chans)  19 us
    dot_general x1, matrix products, body(): lax.dot_general(patches, dpre, (((0,), (0,)), ((), ())), preferred_elemen...  16 us
  transfers between devices with their start and end apart: 5, of which 4 were waited for; matrix products, arithmetic and copies ran while one was open for 1% of the time, Pallas kernels for 0%

commit v1 on v0

v1 whole, which is shorter than its diff:
```python
import functools

import jax
import jax.numpy as jnp
import numpy as np
from jax import lax
from jax.experimental import pallas as pl
from jax.experimental.pallas import tpu as pltpu
from jax.sharding import PartitionSpec as P

F32 = jnp.float32
B16 = jnp.bfloat16
COLS = 24
LIMIT = 56 * 1024 * 1024
NT = (((1,), (1,)), ((), ()))
TN = (((0,), (0,)), ((), ()))


def dot(a, b, dims=None):
    if dims is None:
        return jnp.dot(a, b, preferred_element_type=F32)
    return lax.dot_general(a, b, dims, preferred_element_type=F32)


def call(kernel, outs, scratch=(), **kw):
    params = pltpu.CompilerParams(vmem_limit_bytes=LIMIT)
    return pl.pallas_call(kernel, out_shape=outs, scratch_shapes=list(scratch), compiler_params=params, **kw)


def smem():
    return pl.BlockSpec(memory_space=pltpu.SMEM)


def vmem():
    return pl.BlockSpec(memory_space=pltpu.VMEM)


def pack_tables(chans, run, ny, nz):
    half = chans // 2
    lane = np.arange(half)
    into = np.zeros((2, 2, chans, chans), np.float32)
    for core in range(2):
        channel = (lane // run) * 2 * run + core * run + lane % run
        for side in range(2):
            into[core, side, channel, side * half + lane] = 1
    block = wide(run) * nz
    place = (lane // run // nz) * block + (lane % run) * nz + lane // run % nz
    back = np.zeros((2, chans, ny * block), np.float32)
    for side in range(2):
        back[side, side * half + lane, place] = 1
    direct = np.zeros((2, chans, ny * block), np.float32)
    for core in range(2):
        direct[core, (lane // run) * 2 * run + core * run + lane % run, place] = 1
    return into, back, direct


def wide(run):
    return -(-run // 8) * 8


def first_kernel(at_ref, x_ref, into_ref, own_ref, oth_ref, tail_ref, past_ref, top_ref, bot_ref, ptop_ref, pbot_ref):
    c = at_ref[0]
    nf, band, chans = x_ref.shape
    for pair in range(nf // 2):
        a, b = x_ref[2 * pair], x_ref[2 * pair + 1]
        own_ref[pair] = (dot(a, into_ref[c, 0]) + dot(b, into_ref[c, 1])).astype(B16)
        oth_ref[pair] = (dot(a, into_ref[1 - c, 0]) + dot(b, into_ref[1 - c, 1])).astype(B16)
    tail_ref[0] = own_ref[nf // 2 - 1]
    past_ref[...] = x_ref[nf - 2 :]
    for f in range(nf):
        wide_frame = x_ref[f].astype(F32)
        top = wide_frame[:COLS].astype(B16)
        bot = wide_frame[band - COLS :].astype(B16)
        top_ref[f] = top
        bot_ref[f] = bot
        if f >= nf - 2:
            ptop_ref[f - nf + 2] = top
            pbot_ref[f - nf + 2] = bot


def merge_kernel(at_ref, own_ref, got_ref, past_ref, sent_ref, into_ref, out_ref):
    c = at_ref[0]

    @pl.when(c == 0)
    def _():
        out_ref[0] = (dot(past_ref[0], into_ref[0, 0]) + dot(past_ref[1], into_ref[0, 1])).astype(B16)
        out_ref[1:3] = own_ref[...]
        out_ref[3:5] = got_ref[...]

    @pl.when(c == 1)
    def _():
        out_ref[0] = sent_ref[0]
        out_ref[1:3] = got_ref[...]
        out_ref[3:5] = own_ref[...]


def unpack_kernel(at_ref, a0, a1, a2, a3, back_ref, out_ref):
    x = at_ref[1]
    pair = pl.program_id(0)
    band = a0.shape[1]
    for d, ref in enumerate((a0, a1, a2, a3)):
        at = pl.multiple_of(lax.rem(x - d + 4, 4) * band, band)
        for side in range(2):
            out_ref[side, pl.ds(at, band), :] = dot(ref[0], back_ref[side]).astype(B16)


def forward_kernel(at_ref, pos_ref, x_ref, past_ref, top_ref, bot_ref, ptop_ref, pbot_ref, w_ref, hw_ref,
                   pre_ref, lat_ref, kf_ref, wide_ref):
    step = pl.program_id(0)
    nf, band, chans = x_ref.shape
    rows = band + 2 * COLS

    @pl.when(step == 0)
    def _():
        col = lax.rem(lax.broadcasted_iota(jnp.int32, (rows, 1), 0), COLS)
        for f in range(nf + 2):
            if f < 2:
                parts = (ptop_ref[f], past_ref[f], pbot_ref[f])
            else:
                parts = (top_ref[f - 2], x_ref[f - 2], bot_ref[f - 2])
            v = jnp.concatenate([p.astype(F32) for p in parts], axis=0)
            for dw in range(3):
                if dw == 0:
                    s = jnp.where(col > 0, pltpu.roll(v, 1, 0), 0.0)
                elif dw == 2:
                    s = jnp.where(col < COLS - 1, pltpu.roll(v, rows - 1, 0), 0.0)
                else:
                    s = v
                for dh in range(3):
                    wide_ref[dh, f * band : (f + 1) * band, dw * chans : (dw + 1) * chans] = s[
                        dh * COLS : dh * COLS + band
                    ].astype(B16)

    dt, dh = step // 3, lax.rem(step, 3)
    part = dot(wide_ref[dh, pl.ds(pl.multiple_of(dt * band, band), nf * band), :], w_ref[0])
    for f in range(nf):
        keep = jnp.where(pos_ref[f] >= 2 - dt, 1.0, 0.0)
        piece = keep * part[f * band : (f + 1) * band]

        @pl.when(step == 0)
        def _():
            pre_ref[f * band : (f + 1) * band] = piece

        @pl.when(step > 0)
        def _():
            pre_ref[f * band : (f + 1) * band] += piece

    @pl.when(step == 8)
    def _():
        zdim = lat_ref.shape[1] // 2
        row = lax.broadcasted_iota(jnp.int32, kf_ref.shape, 0)
        kf = jnp.zeros(kf_ref.shape, F32)
        for f in range(nf):
            pre = pre_ref[f * band : (f + 1) * band]
            act = (pre * (1.0 / (1.0 + jnp.exp(-pre)))).astype(B16)
            lat = dot(act, hw_ref[...])
            lat_ref[f * band : (f + 1) * band] = lat
            lane = lax.broadcasted_iota(jnp.int32, lat.shape, 1)
            term = jnp.where(lane < zdim, lat * lat, jnp.exp(lat) - 1.0 - lat)
            kf = jnp.where(row == at_ref[0] * nf + f, 0.5 * jnp.sum(term), kf)
        kf_ref[...] = kf


def back_kernel(per_frame, at_ref, pre_ref, lat_ref, hw_ref, left_ref, mid_ref, right_ref, same_ref, lens_ref,
                d0, d1, d2, d3, k_ref, g_ref, grad_ref, turned_ref, head_ref):
    c, x = at_ref[0], at_ref[1]
    cells, chans = pre_ref.shape
    nf = g_ref.shape[0] // 2
    band = cells // nf
    per = g_ref.shape[0]
    window = jnp.concatenate(
        [left_ref[0], left_ref[1], left_ref[2], mid_ref[...], right_ref[0], right_ref[1], right_ref[2]], axis=0
    )
    row = lax.broadcasted_iota(jnp.int32, g_ref.shape, 0)
    total = jnp.zeros(g_ref.shape, F32)
    for f in range(per):
        total = jnp.where(row == f, jnp.sum(same_ref[:, f : f + 1] * window, axis=0, keepdims=True), total)
    k_ref[...] = total
    g_ref[...] = lens_ref[...] / (lens_ref[...] * per_frame + total)
    head = jnp.zeros(head_ref.shape, F32)
    for f in range(nf):
        at = slice(f * band, (f + 1) * band)
        lat = lat_ref[at]
        zdim = lat.shape[1] // 2
        g = g_ref[pl.ds(c * nf + f, 1), :][:, : 2 * zdim]
        lane = lax.broadcasted_iota(jnp.int32, lat.shape, 1)
        dlat = (g * jnp.where(lane < zdim, lat, 0.5 * (jnp.exp(lat) - 1.0))).astype(B16)
        dact = dot(dlat, hw_ref[...], NT)
        pre = pre_ref[at]
        sig = 1.0 / (1.0 + jnp.exp(-pre))
        dpre = (dact * sig * (1.0 + pre * (1.0 - sig))).astype(B16)
        act = (pre * sig).astype(B16)
        head = head + dot(dlat, act, TN)
        grad_ref[at] = dpre.astype(F32)
    head_ref[...] = head
    turned_ref[...] = jnp.transpose(grad_ref[...], (1, 0)).astype(B16)
    block = chans // 4
    hblock = head_ref.shape[0] // 4
    for d, ref in enumerate((d0, d1, d2, d3)):
        to = lax.rem(x + d, 4)
        ref[:block] = turned_ref[pl.ds(pl.multiple_of(to * block, block), block), :]
        part = head_ref[pl.ds(pl.multiple_of(to * hblock, hblock), hblock), :]
        high = part.astype(B16).astype(F32)
        both = jnp.concatenate([high, part - high], axis=0)
        if cells > chans:
            both = jnp.concatenate([both, jnp.zeros((2 * hblock, cells - chans), F32)], axis=1)
        ref[block:] = both.astype(B16)


def weight_kernel(ny, at_ref, keep_ref, loss_ref, a0, a1, a2, a3, b0, b1, b2, b3, x_ref, direct_ref,
                  *refs):
    sends, (held_ref, taps_ref, acc_ref, out_ref) = refs[:ny], refs[ny:]
    c, x, y = at_ref[0], at_ref[1], at_ref[2]
    full = x_ref.shape[1]
    band = full // 4
    block = taps_ref.shape[0] // 9
    chans = direct_ref.shape[1]
    lanes = acc_ref.shape[2]
    hsum = jnp.zeros((2 * ((held_ref.shape[2] - block) // 2), chans), F32)
    for core, given in ((c, (a0, a1, a2, a3)), (1 - c, (b0, b1, b2, b3))):
        for d, ref in enumerate(given):
            held_ref[core, lax.rem(x - d + 4, 4)] = ref[...]
            hsum = hsum + ref[block:, :chans].astype(F32)
    hblock = hsum.shape[0] // 2
    acc_ref[...] = jnp.zeros(acc_ref.shape, F32)
    lane = lax.broadcasted_iota(jnp.int32, (1, full), 1)
    col = lax.rem(lane, COLS)
    line = lane // COLS

    def core_frames(core, carry):
        for lf in range(4):
            frame = jnp.zeros((block, full), F32)
            for xs in range(4):
                v = held_ref[core, xs, :block, :].astype(F32)
                shift = ((xs - lf) * band) % full
                if shift:
                    v = pltpu.roll(v, shift, 1)
                frame = jnp.where(lane // band == xs, v, frame)
            for dw in range(3):
                if dw == 0:
                    v = jnp.where(col < COLS - 1, pltpu.roll(frame, full - 1, 1), 0.0)
                elif dw == 2:
                    v = jnp.where(col > 0, pltpu.roll(frame, 1, 1), 0.0)
                else:
                    v = frame
                for dh in range(3):
                    if dh == 0:
                        s = jnp.where(line < full // COLS - 1, pltpu.roll(v, full - COLS, 1), 0.0)
                    elif dh == 2:
                        s = jnp.where(line > 0, pltpu.roll(v, COLS, 1), 0.0)
                    else:
                        s = v
                    q = dh * 3 + dw
                    taps_ref[q * block : (q + 1) * block, :] = s.astype(B16)
            f = core * 4 + lf
            for dt in range(3):
                acc_ref[dt, : 9 * block] += keep_ref[f * 3 + dt] * dot(taps_ref[...], x_ref[f + dt])
        return carry

    lax.fori_loop(0, 2, core_frames, 0)
    direct = direct_ref[c]
    both = hsum[:hblock] + hsum[hblock:]
    high = both.astype(B16)
    low = (both - high.astype(F32)).astype(B16)
    acc_ref[0, 9 * block : 9 * block + hblock] = dot(high, direct) + dot(low, direct)
    loss = jnp.full((8, lanes), loss_ref[0], F32)
    top = loss.astype(B16).astype(F32)
    mid = (loss - top).astype(B16).astype(F32)
    acc_ref[1, 9 * block : 9 * block + 8] = top
    acc_ref[1, 9 * block + 8 : 9 * block + 16] = mid
    acc_ref[1, 9 * block + 16 : 9 * block + 24] = loss - top - mid
    rows = sends[0].shape[1]
    ystep = lanes // ny
    for dt in range(3):
        out_ref[...] = jnp.transpose(acc_ref[dt], (1, 0))
        for d, ref in enumerate(sends):
            to = lax.rem(y + d, ny)
            ref[dt] = out_ref[pl.ds(pl.multiple_of(to * ystep, 8), rows), :].astype(ref.dtype)


def add_kernel(ny, nz, run, at_ref, *refs):
    gets, sends, (sum_ref, part_ref) = refs[:ny], refs[ny : ny + nz], refs[ny + nz :]
    total = gets[0][...]
    for ref in gets[1:]:
        total = total + ref[...].astype(F32)
    chunk = sum_ref.shape[3]
    for i in range(sum_ref.shape[0]):
        sum_ref[i] = total[:, :, i * chunk : (i + 1) * chunk]
    part_ref[...] = jnp.zeros(part_ref.shape, F32)
    step = part_ref.shape[1] // 3
    for z in range(nz):
        for dt in range(3):
            for i in range(sum_ref.shape[0]):
                part_ref[z, dt * step : dt * step + run, i * chunk : (i + 1) * chunk] = sum_ref[
                    i, dt, pl.ds(z, run, stride=nz), :
                ]
    for d, ref in enumerate(sends):
        ref[...] = part_ref[lax.rem(at_ref[3] + d, nz)].astype(ref.dtype)


def last_kernel(*refs):
    total = refs[0][...]
    for ref in refs[1:-1]:
        total = total + ref[...].astype(F32)
    refs[-1][...] = total


def body(frames, conv_weight, head_weight, clip_len):
    nf, nrow, ncol, chans = frames.shape
    band = nrow * ncol
    cells = nf * band
    count = lax.axis_size("tm")
    ny = 4 if count == 64 else 2
    nz = count // 2 // ny
    run = chans // count
    chip = 2 * nf
    t, x = lax.axis_index("tm"), lax.axis_index("space")
    c, k = t % 2, t // 2
    y, z = k // nz, k % nz
    at = jnp.stack([c, x, y, z]).astype(jnp.int32)
    shape = jax.ShapeDtypeStruct

    def index(yy, zz, cc):
        return ((yy % ny) * nz + zz % nz) * 2 + cc

    every = [(yy, zz, cc) for yy in range(ny) for zz in range(nz) for cc in range(2)]

    def over_core(v):
        return lax.ppermute(v, "tm", [(i, i ^ 1) for i in range(count)])

    def over_chip(v, d):
        return lax.ppermute(v, "tm", [(i, (i + 2 * d) % count) for i in range(count)])

    def over_x(v, d):
        return lax.ppermute(v, "space", [(i, (i + d) % 4) for i in range(4)])

    def over_y(v, d):
        return lax.ppermute(v, "tm", [(index(a, b, e), index(a + d, b, e)) for a, b, e in every])

    def over_z(v, d):
        return lax.ppermute(v, "tm", [(index(a, b, e), index(a, b + d, e)) for a, b, e in every])

    nclip = clip_len.shape[0]
    order = jnp.arange(nclip)
    ends = jnp.sum(jnp.where(order[None, :] <= order[:, None], clip_len[None, :], 0), axis=1)
    ids = chip * k + jnp.arange(-3 * chip, 4 * chip)
    clip = jnp.where(ids < 0, -1, jnp.sum(ends[None, :] <= ids[:, None], axis=1))
    mine = clip[3 * chip : 4 * chip]
    same = (clip[:, None] == mine[None, :]).astype(F32)
    member = mine[:, None] == order[None, :]
    lens = jnp.sum(jnp.where(member, clip_len[None, :], 0), axis=1)
    pos = ids[3 * chip : 4 * chip] - jnp.sum(jnp.where(member, (ends - clip_len)[None, :], 0), axis=1)
    lens = lens.astype(F32)
    keep = (pos[:, None] >= jnp.array([2, 1, 0])[None, :]).astype(F32).reshape(-1)
    own_pos = lax.dynamic_slice_in_dim(pos, c * nf, nf).astype(jnp.int32)

    into, back, direct = (jnp.asarray(v, B16) for v in pack_tables(chans, run, ny, nz))
    flat = frames.reshape(nf, band, chans)
    pairs = nf // 2
    own, oth, tail, past, top, bot, ptop, pbot = call(
        first_kernel,
        [shape((pairs, band, chans), B16)] * 2
        + [shape((1, band, chans), B16), shape((2, band, chans), B16)]
        + [shape((nf, ncol, chans), B16)] * 2
        + [shape((2, ncol, chans), B16)] * 2,
        in_specs=[smem(), vmem(), vmem()],
        name="first",
    )(at, flat, into)
    both = ("tm", "space")
    past = lax.ppermute(past, "tm", [(i, i + 1) for i in range(count - 1)])
    top, bot = (
        lax.ppermute(bot, "space", [(i, i + 1) for i in range(3)]),
        lax.ppermute(top, "space", [(i + 1, i) for i in range(3)]),
    )
    ptop, pbot = (
        lax.ppermute(pbot, both, [(4 * i + j, 4 * (i + 1) + j + 1) for i in range(count - 1) for j in range(3)]),
        lax.ppermute(ptop, both, [(4 * i + j + 1, 4 * (i + 1) + j) for i in range(count - 1) for j in range(3)]),
    )
    got = over_core(oth)
    sent = lax.ppermute(tail, "tm", [(i, i + 2) for i in range(1, count - 2, 2)])
    five = call(
        merge_kernel,
        shape((5, band, chans), B16),
        in_specs=[smem()] + [vmem()] * 5,
        name="merge",
    )(at, own, got, past, sent, into)
    fives = [five] + [over_x(five, d) for d in (1, 2, 3)]

    whole = lambda *dims: pl.BlockSpec(dims, lambda i: (0,) * len(dims))
    zlat = head_weight.shape[1]
    pre, latent, kframe = call(
        forward_kernel,
        [shape((cells, chans), F32), shape((cells, zlat), F32), shape((chip, 128), F32)],
        [pltpu.VMEM((3, (nf + 2) * band, 3 * chans), B16)],
        grid=(9,),
        in_specs=[smem(), smem()]
        + [whole(*v.shape) for v in (flat, past, top, bot, ptop, pbot)]
        + [pl.BlockSpec((1, 3 * chans, chans), lambda i: (i, 0, 0)), whole(chans, zlat)],
        out_specs=[whole(cells, chans), whole(cells, zlat), whole(chip, 128)],
        name="forward",
    )(at, own_pos, flat, past, top, bot, ptop, pbot, conv_weight.reshape(9, 3 * chans, chans), head_weight)

    xs = call(
        unpack_kernel,
        shape((10, 4 * band, back.shape[2]), B16),
        grid=(5,),
        in_specs=[smem()] + [pl.BlockSpec((1, band, chans), lambda i: (i, 0, 0))] * 4 + [whole(*back.shape)],
        out_specs=pl.BlockSpec((2, 4 * band, back.shape[2]), lambda i: (i, 0, 0)),
        name="unpack",
    )(at, *fives, back)

    kchip = kframe + over_core(kframe)
    kchip = kchip + over_x(kchip, 1) + over_x(kchip, 2) + over_x(kchip, 3)
    triple = jnp.stack([over_chip(kchip, 1), kchip, over_chip(kchip, -1)])
    left, right = over_chip(triple, 2), over_chip(triple, -2)
    per_frame = float(4 * band)
    hblock = zlat // 4
    block = chans // 4
    message = shape((block + 2 * hblock, cells), B16)
    lens_rows = jnp.broadcast_to(lens[:, None], (chip, 128))
    *mine_d, totals = call(
        functools.partial(back_kernel, per_frame),
        [message] * 4 + [shape((chip, 128), F32)],
        [
            pltpu.VMEM((chip, 128), F32),
            pltpu.VMEM((cells, chans), F32),
            pltpu.VMEM((chans, cells), B16),
            pltpu.VMEM((zlat, chans), F32),
        ],
        in_specs=[smem()] + [vmem()] * 8,
        name="back",
    )(at, pre, latent, head_weight, left, kchip, right, same, lens_rows)
    first = (pos == 0).astype(F32)
    loss_part = jnp.sum(first * lens * jnp.log1p(totals[:, 0] / (lens * per_frame)))
    mine_d = [mine_d[0]] + [over_x(mine_d[d], d) for d in (1, 2, 3)]
    core_d = [over_core(v) for v in mine_d]

    lanes = back.shape[2]
    rows = run * nz
    wrow = 9 * block + 32
    sends = call(
        functools.partial(weight_kernel, ny),
        [shape((3, rows, wrow), F32)] + [shape((3, rows, wrow), B16)] * (ny - 1),
        [
            pltpu.VMEM((2, 4) + message.shape, B16),
            pltpu.VMEM((9 * block, 4 * band), B16),
            pltpu.VMEM((3, wrow, lanes), F32),
            pltpu.VMEM((lanes, wrow), F32),
        ],
        in_specs=[smem()] * 3 + [vmem()] * 10,
        name="weight",
    )(at, keep, loss_part[None], *mine_d, *core_d, xs, direct)
    gets = [sends[0]] + [over_y(sends[d], d) for d in range(1, ny)]
    step = wide(run)
    chunk = 128 if wrow % 128 == 0 else wrow
    parts = call(
        functools.partial(add_kernel, ny, nz, run),
        [shape((3 * step, wrow), F32)] * nz,
        [pltpu.VMEM((wrow // chunk, 3, rows, chunk), F32), pltpu.VMEM((nz, 3 * step, wrow), F32)],
        in_specs=[smem()] + [vmem()] * ny,
        name="add",
    )(at, *gets)
    parts = [parts[0]] + [over_z(parts[d], d) for d in range(1, nz)]
    total = call(last_kernel, shape((3 * step, wrow), F32), name="last")(*parts)
    total = total.reshape(3, step, wrow)
    weight_grad = total[:, :run, : 9 * block].reshape(3, run, 9, block).transpose(0, 2, 1, 3).reshape(27, run, block)
    base = 9 * block
    head_grad = total[0, :run, base : base + hblock]
    loss = total[1, 0, base] + total[1, 0, base + 8] + total[1, 0, base + 16]
    return latent.reshape(nf, nrow, ncol, zlat), loss, weight_grad, head_grad


def solution(mesh):
    in_specs = (P("tm", "space", None, None), P(), P(), P())
    out_specs = (P("tm", "space", None, None), P(), P(None, "tm", "space"), P("tm", "space"))
    return jax.shard_map(body, mesh=mesh, in_specs=in_specs, out_specs=out_specs, check_vma=False)
```

time: 614 us -> 196 us (0.32)
  blocking collectives: 337 us -> 0 us
  waiting for transfers between devices: 174 us -> 59.6 us
  starting transfers between devices: 6.69 us -> 60.9 us
  Pallas kernels: 0 us -> 52.3 us
  matrix products: 35.8 us -> 0 us
  local copies, waits for them, and re-layouts: 32.7 us -> 13.2 us
  between operations: 15.7 us -> 4.09 us
    unnamed x2 -> x0, blocking collectives: 258 us -> none
    reduce_scatter x2 -> x0, waiting for transfers between devices: 164 us -> none  [the longest x1 164 us: body(): lax.psum_scatter(weight_part, 'space', scatter_dimension=2, tiled=True)]
    psum x1 -> x0, blocking collectives: 78.1 us -> none  [body(): totals = lax.psum(partial_sums, ('tm', 'space'))]
    ppermute x3 -> x35, starting transfers between devices: 6.61 us -> 60.9 us  [the longest x7 15.7 us: over_z(): lax.ppermute(v, 'tm', [(index(a, b, e), index(a, b + d, e)) for a, b, e i...]
    pallas_call x0 -> x8, Pallas kernels: none -> 52.3 us  [the longest x1 16.3 us: body(): call(forward_kernel, [shape((cells, chans), F32), shape((cells, zlat), F3...]
    ppermute x3 -> x35, waiting for transfers between devices: 9.68 us -> 59.6 us  [the longest x9 30.1 us: over_x(): return lax.ppermute(v, 'space', [(i, (i + d) % 4) for i in range(4)])]
    dot_general x4 -> x0, matrix products: 35.8 us -> none  [the longest x1 19.3 us: body(): jnp.dot(patches, conv_weight.reshape(27 * chans, chans), preferred_elemen...]
    reshape x1, local copies, waits for them, and re-layouts: 19 us -> 0.98 us  [body(): total[:, :run, :9 * block].reshape(3, run, 9, block).transpose(0, 2, 1, 3)]
  transfers between devices with their start and end apart: 5 -> 35, of which waited for: 4 -> 15; matrix products, arithmetic and copies ran while one was open for 1% -> 4% of each run, Pallas kernels for 0% -> 15%
where the time goes in v1:
time: 196 us; the launch traced here: 195 us
  starting transfers between devices  60.9 us (31%)
  waiting for transfers between devices  59.6 us (30%)
  Pallas kernels  52.3 us (27%)
  local copies, waits for them, and re-layouts  13.2 us (7%)
  other arithmetic  5.18 us (3%)
  between operations  4.09 us (2%)
    ppermute x9, waiting for transfers between devices, over_x(): return lax.ppermute(v, 'space', [(i, (i + d) % 4) for i in range(4)])  30.1 us
    pallas_call x1, Pallas kernels, body(): call(forward_kernel, [shape((cells, chans), F32), shape((cells, zlat), F3...  16.3 us
    ppermute x7, starting transfers between devices, over_z(): lax.ppermute(v, 'tm', [(index(a, b, e), index(a, b + d, e)) for a, b, e i...  15.7 us
    pallas_call x1, Pallas kernels, body(): call(functools.partial(weight_kernel, ny), [shape((3, rows, wrow), F32)]...  15.5 us
    ppermute x9, starting transfers between devices, over_x(): return lax.ppermute(v, 'space', [(i, (i + d) % 4) for i in range(4)])  12.3 us
    ppermute x7, waiting for transfers between devices, over_z(): lax.ppermute(v, 'tm', [(index(a, b, e), index(a, b + d, e)) for a, b, e i...  11.5 us
    ppermute x3, waiting for transfers between devices, over_y(): lax.ppermute(v, 'tm', [(index(a, b, e), index(a + d, b, e)) for a, b, e i...  10.9 us
    ppermute x4, starting transfers between devices, over_chip(): lax.ppermute(v, 'tm', [(i, (i + 2 * d) % count) for i in range(count)])  9.63 us
  transfers between devices with their start and end apart: 35, of which 15 were waited for; matrix products, arithmetic and copies ran while one was open for 4% of the time, Pallas kernels for 15%

profile of v1, /device:TPU:32, one launch (start us, length us, event | category | flops | bytes accessed | tf_op | source)
XLA Modules:
  0.0 195.3 jit_solution(5278549613490499610)
XLA Ops:
  1.3 3.3 %first.1 = (bf16[2,192,384]{2,1,0:T(8,128)(2,1)}, bf16[2,192,384]{2,1,0:T(8,128)(2,1)}, bf16[1,192,384]{2,1,0:T(8,128)(2,1)}, bf16[2,192,384]{2,1,0:T(8,128)(2,1...) custom-call(s32[4]{0:T(128)} %pad_add_fusion.at_ref, ...), custom_call_target="tpu_custom_call" | custom-call | tf_op jit(solution)/shard_map/first/pallas_call | solution.py:360
  4.6 1.9 collective-permute-start
  6.5 2.1 %collective-permute-start.20 = (bf16[2,192,384]{2,1,0:T(8,128)(2,1)}, bf16[2,192,384]{2,1,0:T(8,128)(2,1)S(1)}, u32[]{:S(2)}, u32[]{:S(2)}) collective-permute-start(bf16[2,192,384]{2,1,0:T(8,128)(2,1)} %get-tuple-element.46), channel_id=1, source_target_pairs={{0,4},{4,0},{8,12},{12,8},{16,20},{20,16},{24,28},{28,24},{32,36},... | collective-permute-start | bytes 884744 | tf_op jit(solution)/shard_map/ppermute | solution.py:329
  8.6 3.4 %collective-permute-start.1 = (bf16[4,24,384]{2,1,0:T(8,128)(2,1)}, bf16[4,24,384]{2,1,0:T(8,128)(2,1)S(1)}, u32[]{:S(2)}, u32[]{:S(2)}) collective-permute-start(bf16[4,24,384]{2,1,0:T(8,128)(2,1)} %get-tuple-element.33), channel_id=1, source_target_pairs={{0,1},{1,2},{2,3},{4,5},{5,6},{6,7},{8,9},{9,10},{10,11},{12,13},{... | collective-permute-start | bytes 221192 | tf_op jit(solution)/shard_map/ppermute | solution.py:372
  13.3 3.6 %collective-permute-start.3 = (bf16[2,24,384]{2,1,0:T(8,128)(2,1)}, bf16[2,24,384]{2,1,0:T(8,128)(2,1)S(1)}, u32[]{:S(2)}, u32[]{:S(2)}) collective-permute-start(bf16[2,24,384]{2,1,0:T(8,128)(2,1)} %get-tuple-element.35), channel_id=1, source_target_pairs={{0,5},{1,6},{2,7},{4,9},{5,10},{6,11},{8,13},{9,14},{10,15},{12,17... | collective-permute-start | bytes 110600 | tf_op jit(solution)/shard_map/ppermute | solution.py:376
  22.8 3.4 %collective-permute-done.4.pbot_ref = bf16[2,24,384]{2,1,0:T(8,128)(2,1)S(1)} collective-permute-done((bf16[2,24,384]{2,1,0:T(8,128)(2,1)}, bf16[2,24,384]{2,1,0:T(8,128)(2,1)S(1)}, u32[]{:S(2)}, u32[]{:S(2)}) %collective-permute-start.4) | collective-permute-done | bytes 36896 | tf_op jit(solution)/shard_map/ppermute | solution.py:377
  27.0 16.3 %forward.1 = (f32[768,384]{1,0:T(8,128)}, f32[768,32]{1,0:T(8,128)}, f32[8,128]{1,0:T(8,128)}) custom-call(s32[4]{0:T(128)} %pad_add_fusion.at_ref, s32[4]{0:T(128)} %dynamic_slice.3.pos_ref, bf16[4,192,384]{2,1,0:T(8,128)(2,1)} %bitcast.20, bf16[2,192,384]{2,1,0:T(8,128)(2,1)} %copy-done, bf16[4,24,384]{2,1,0:T(8,128)(2,1)} %copy-done.23, ...), custom_call_target="tpu_custom_call" | custom-call | tf_op jit(solution)/shard_map/forward/pallas_call | solution.py:391
  46.2 1.7 collective-permute-start.6
  47.9 2.3 %collective-permute-start.7 = (f32[8,128]{1,0:T(8,128)S(1)}, f32[8,128]{1,0:T(8,128)S(1)}, u32[]{:S(2)}, u32[]{:S(2)}) collective-permute-start(f32[8,128]{1,0:T(8,128)S(1)} %add.68), channel_id=1, source_target_pairs={{0,2},{1,3},{2,0},{3,1},{4,6},{5,7},{6,4},{7,5},{8,10},{9,11},{10,... | collective-permute-start | bytes 12296 | tf_op jit(solution)/shard_map/ppermute | solution.py:335
  50.2 1.9 collective-permute-start.8
  53.9 3.1 %collective-permute-start.9 = (f32[8,128]{1,0:T(8,128)S(1)}, f32[8,128]{1,0:T(8,128)S(1)}, u32[]{:S(2)}, u32[]{:S(2)}) collective-permute-start(f32[8,128]{1,0:T(8,128)S(1)} %add_add_fusion.mid_ref), channel_id=1, source_target_pairs={{0,8},{4,12},{8,16},{12,20},{16,24},{20,28},{24,32},{28,36},{32,40... | collective-permute-start | bytes 12296 | tf_op jit(solution)/shard_map/ppermute | solution.py:332
  57.8 2.8 %merge.1.a0 = bf16[5,192,384]{2,1,0:T(8,128)(2,1)} custom-call(s32[4]{0:T(128)} %pad_add_fusion.at_ref, bf16[2,192,384]{2,1,0:T(8,128)(2,1)} %get-tuple-element.45.own_ref, bf16[2,192,384]{2,1,0:T(8,128)(2,1)} %copy-done.4, bf16[2,192,384]{2,1,0:T(8,128)(2,1)} %copy-done, bf16[1,192,384]{2,1,0:T(8,128)(2,1)} %copy-done.15, ...), custom_call_target="tpu_custom_call" | custom-call | tf_op jit(solution)/shard_map/merge/pallas_call | solution.py:381
  60.8 3.8 %collective-permute-start.23 = (bf16[5,192,384]{2,1,0:T(8,128)(2,1)}, bf16[5,192,384]{2,1,0:T(8,128)(2,1)S(1)}, u32[]{:S(2)}, u32[]{:S(2)}) collective-permute-start(bf16[5,192,384]{2,1,0:T(8,128)(2,1)} %merge.1.a0), channel_id=1, source_target_pairs={{0,2},{1,3},{2,0},{3,1},{4,6},{5,7},{6,4},{7,5},{8,10},{9,11},{10,... | collective-permute-start | bytes 2211848 | tf_op jit(solution)/shard_map/ppermute | solution.py:335
  64.9 5.3 %collective-permute-start.11 = (f32[3,8,128]{2,1,0:T(8,128)S(1)}, f32[3,8,128]{2,1,0:T(8,128)S(1)}, u32[]{:S(2)}, u32[]{:S(2)}) collective-permute-start(f32[3,8,128]{2,1,0:T(8,128)S(1)} %pad_maximum_fusion), channel_id=1, source_target_pairs={{0,16},{4,20},{8,24},{12,28},{16,32},{20,36},{24,40},{28,44},{32,4... | collective-permute-start | bytes 36872 | tf_op jit(solution)/shard_map/ppermute | solution.py:332
  75.4 3.3 %back.1 = (bf16[112,768]{1,0:T(8,128)(2,1)}, bf16[112,768]{1,0:T(8,128)(2,1)}, bf16[112,768]{1,0:T(8,128)(2,1)}, bf16[112,768]{1,0:T(8,128)(2,1)}, f32[8,128]{1,0:T(8,128)}) custom-call(s32[4]{0:T(128)} %pad_add_fusion.at_ref, f32[768,384]{1,0:T(8,128)} %get-tuple-element.38.pre_ref, f32[768,32]{1,0:T(8,128)} %get-tuple-element.37.lat_ref, ...), custom_call_target="tpu_custom_call" | custom-call | tf_op jit(solution)/shard_map/back/pallas_call | solution.py:421
  78.8 2.0 %collective-permute-start.13 = (bf16[112,768]{1,0:T(8,128)(2,1)}, bf16[112,768]{1,0:T(8,128)(2,1)S(1)}, u32[]{:S(2)}, u32[]{:S(2)}) collective-permute-start(bf16[112,768]{1,0:T(8,128)(2,1)} %get-tuple-element.42), channel_id=1, source_target_pairs={{0,1},{1,2},{2,3},{3,0},{4,5},{5,6},{6,7},{7,4},{8,9},{9,10},{10,1... | collective-permute-start | bytes 516104 | tf_op jit(solution)/shard_map/ppermute | solution.py:335
  80.8 23.5 %collective-permute-done.13.a1 = bf16[112,768]{1,0:T(8,128)(2,1)S(1)} collective-permute-done((bf16[112,768]{1,0:T(8,128)(2,1)}, bf16[112,768]{1,0:T(8,128)(2,1)S(1)}, u32[]{:S(2)}, u32[]{:S(2)}) %collective-permute-start.13) | collective-permute-done | bytes 172064 | tf_op jit(solution)/shard_map/ppermute | solution.py:335
  105.0 5.6 %collective-permute-done.15.a3 = bf16[112,768]{1,0:T(8,128)(2,1)S(1)} collective-permute-done((bf16[112,768]{1,0:T(8,128)(2,1)}, bf16[112,768]{1,0:T(8,128)(2,1)S(1)}, u32[]{:S(2)}, u32[]{:S(2)}) %collective-permute-start.15) | collective-permute-done | bytes 172064 | tf_op jit(solution)/shard_map/ppermute | solution.py:335
  113.5 6.8 %unpack.1.x_ref = bf16[10,768,256]{2,1,0:T(8,128)(2,1)} custom-call(s32[4]{0:T(128)} %pad_add_fusion.at_ref, bf16[5,192,384]{2,1,0:T(8,128)(2,1)} %merge.1.a0, bf16[5,192,384]{2,1,0:T(8,128)(2,1)} %copy-done.1, bf16[5,192,384]{2,1,0:T(8,128)(2,1)} %copy-done.2, bf16[5,192,384]{2,1,0:T(8,128)(2,1)} %copy-done.3, bf16[2,384,256]{2,1,0:T(8,128)(2,1)} %constant.75.clone.back_ref), custom_call_target="tpu_custom_call" | custom-call | tf_op jit(solution)/shard_map/unpack/pallas_call | solution.py:403
  121.2 15.5 %weight.1 = (f32[3,48,896]{2,1,0:T(8,128)}, bf16[3,48,896]{2,1,0:T(8,128)(2,1)}, bf16[3,48,896]{2,1,0:T(8,128)(2,1)}, bf16[3,48,896]{2,1,0:T(8,128)(2,1)}) custom-call(s32[4]{0:T(128)} %pad_add_fusion.at_ref, f32[24]{0:T(128)} %reshape.61.keep_ref, f32[1]{0:T(128)} %bitcast.10.loss_ref, bf16[112,768]{1,0:T(8,128)(2,1)} %get-tuple-element.41.a0, ...), custom_call_target="tpu_custom_call" | custom-call | tf_op jit(solution)/shard_map/weight/pallas_call | solution.py:441
  136.7 3.0 %collective-permute-start.25 = (bf16[3,48,896]{2,1,0:T(8,128)(2,1)}, bf16[3,48,896]{2,1,0:T(8,128)(2,1)S(1)}, u32[]{:S(2)}, u32[]{:S(2)}) collective-permute-start(bf16[3,48,896]{2,1,0:T(8,128)(2,1)} %get-tuple-element.49), channel_id=1, source_target_pairs={{0,64},{4,68},{8,72},{12,76},{16,80},{20,84},{24,88},{28,92},{32,9... | collective-permute-start | bytes 774152 | tf_op jit(solution)/shard_map/ppermute | solution.py:338
  139.7 2.9 %collective-permute-start.26 = (bf16[3,48,896]{2,1,0:T(8,128)(2,1)}, bf16[3,48,896]{2,1,0:T(8,128)(2,1)S(1)}, u32[]{:S(2)}, u32[]{:S(2)}) collective-permute-start(bf16[3,48,896]{2,1,0:T(8,128)(2,1)} %get-tuple-element.50), channel_id=1, source_target_pairs={{0,128},{4,132},{8,136},{12,140},{16,144},{20,148},{24,152},{28,15... | collective-permute-start | bytes 774152 | tf_op jit(solution)/shard_map/ppermute | solution.py:338
  143.9 4.2 %collective-permute-done.25.refs_1_ = bf16[3,48,896]{2,1,0:T(8,128)(2,1)S(1)} collective-permute-done((bf16[3,48,896]{2,1,0:T(8,128)(2,1)}, bf16[3,48,896]{2,1,0:T(8,128)(2,1)S(1)}, u32[]{:S(2)}, u32[]{:S(2)}) %collective-permute-start.25) | collective-permute-done | bytes 258080 | tf_op jit(solution)/shard_map/ppermute | solution.py:338
  148.1 6.7 %collective-permute-done.26.refs_2_ = bf16[3,48,896]{2,1,0:T(8,128)(2,1)S(1)} collective-permute-done((bf16[3,48,896]{2,1,0:T(8,128)(2,1)}, bf16[3,48,896]{2,1,0:T(8,128)(2,1)S(1)}, u32[]{:S(2)}, u32[]{:S(2)}) %collective-permute-start.26) | collective-permute-done | bytes 258080 | tf_op jit(solution)/shard_map/ppermute | solution.py:338
  155.6 2.5 %add.97 = (f32[24,896]{1,0:T(8,128)}, f32[24,896]{1,0:T(8,128)}, f32[24,896]{1,0:T(8,128)}, f32[24,896]{1,0:T(8,128)}, f32[24,896]{1,0:T(8,128)}, /*index=5*/f32...) custom-call(s32[4]{0:T(128)} %pad_add_fusion.at_ref, f32[3,48,896]{2,1,0:T(8,128)} %get-tuple-element.48.refs_0_, ...), custom_call_target="tpu_custom_call" | custom-call | tf_op jit(solution)/shard_map/add/pallas_call | solution.py:456
  159.3 5.6 %collective-permute-start.29 = (f32[24,896]{1,0:T(8,128)}, f32[24,896]{1,0:T(8,128)S(1)}, u32[]{:S(2)}, u32[]{:S(2)}) collective-permute-start(f32[24,896]{1,0:T(8,128)} %get-tuple-element.54), channel_id=1, source_target_pairs={{0,16},{4,20},{8,24},{12,28},{16,32},{20,36},{24,40},{28,44},{32,4... | collective-permute-start | bytes 258056 | tf_op jit(solution)/shard_map/ppermute | solution.py:341
  164.9 3.3 %collective-permute-start.31 = (f32[24,896]{1,0:T(8,128)}, f32[24,896]{1,0:T(8,128)S(1)}, u32[]{:S(2)}, u32[]{:S(2)}) collective-permute-start(f32[24,896]{1,0:T(8,128)} %get-tuple-element.56), channel_id=1, source_target_pairs={{0,32},{4,36},{8,40},{12,44},{16,48},{20,52},{24,56},{28,60},{32,0... | collective-permute-start | bytes 258056 | tf_op jit(solution)/shard_map/ppermute | solution.py:341
  168.2 4.0 %collective-permute-start.32 = (f32[24,896]{1,0:T(8,128)}, f32[24,896]{1,0:T(8,128)S(1)}, u32[]{:S(2)}, u32[]{:S(2)}) collective-permute-start(f32[24,896]{1,0:T(8,128)} %get-tuple-element.57), channel_id=1, source_target_pairs={{0,40},{4,44},{8,48},{12,52},{16,56},{20,60},{24,0},{28,4},{32,8},... | collective-permute-start | bytes 258056 | tf_op jit(solution)/shard_map/ppermute | solution.py:341
  175.0 3.0 %collective-permute-done.30.refs_3_ = f32[24,896]{1,0:T(8,128)S(1)} collective-permute-done((f32[24,896]{1,0:T(8,128)}, f32[24,896]{1,0:T(8,128)S(1)}, u32[]{:S(2)}, u32[]{:S(2)}) %collective-permute-start.30) | collective-permute-done | bytes 86048 | tf_op jit(solution)/shard_map/ppermute | solution.py:341
  178.0 3.7 %collective-permute-done.32.refs_5_ = f32[24,896]{1,0:T(8,128)S(1)} collective-permute-done((f32[24,896]{1,0:T(8,128)}, f32[24,896]{1,0:T(8,128)S(1)}, u32[]{:S(2)}, u32[]{:S(2)}) %collective-permute-start.32) | collective-permute-done | bytes 86048 | tf_op jit(solution)/shard_map/ppermute | solution.py:341
  181.8 2.7 %collective-permute-done.33.refs_6_ = f32[24,896]{1,0:T(8,128)S(1)} collective-permute-done((f32[24,896]{1,0:T(8,128)}, f32[24,896]{1,0:T(8,128)S(1)}, u32[]{:S(2)}, u32[]{:S(2)}) %collective-permute-start.33) | collective-permute-done | bytes 86048 | tf_op jit(solution)/shard_map/ppermute | solution.py:341
  186.0 1.8 last.1
  (136 shorter events, 36.1 us)
Async XLA Ops:
  4.6 21.7 %collective-permute-start = (bf16[2,192,384]{2,1,0:T(8,128)(2,1)}, bf16[2,192,384]{2,1,0:T(8,128)(2,1)S(1)}, u32[]{:S(2)}, u32[]{:S(2)}) collective-permute-start(bf16[2,192,384]{2,1,0:T(8,128)(2,1)} %get-tuple-element.32), channel_id=1, source_target_pairs={{0,4},{4,8},{8,12},{12,16},{16,20},{20,24},{24,28},{28,32},{32,36}... | collective-permute-start | bytes 884744 | tf_op jit(solution)/shard_map/ppermute | solution.py:370
  6.5 50.5 %collective-permute-start.20 = (bf16[2,192,384]{2,1,0:T(8,128)(2,1)}, bf16[2,192,384]{2,1,0:T(8,128)(2,1)S(1)}, u32[]{:S(2)}, u32[]{:S(2)}) collective-permute-start(bf16[2,192,384]{2,1,0:T(8,128)(2,1)} %get-tuple-element.46), channel_id=1, source_target_pairs={{0,4},{4,0},{8,12},{12,8},{16,20},{20,16},{24,28},{28,24},{32,36},... | collective-permute-start | bytes 884744 | tf_op jit(solution)/shard_map/ppermute | solution.py:329
  8.6 17.6 %collective-permute-start.1 = (bf16[4,24,384]{2,1,0:T(8,128)(2,1)}, bf16[4,24,384]{2,1,0:T(8,128)(2,1)S(1)}, u32[]{:S(2)}, u32[]{:S(2)}) collective-permute-start(bf16[4,24,384]{2,1,0:T(8,128)(2,1)} %get-tuple-element.33), channel_id=1, source_target_pairs={{0,1},{1,2},{2,3},{4,5},{5,6},{6,7},{8,9},{9,10},{10,11},{12,13},{... | collective-permute-start | bytes 221192 | tf_op jit(solution)/shard_map/ppermute | solution.py:372
  12.0 14.2 %collective-permute-start.2 = (bf16[4,24,384]{2,1,0:T(8,128)(2,1)}, bf16[4,24,384]{2,1,0:T(8,128)(2,1)S(1)}, u32[]{:S(2)}, u32[]{:S(2)}) collective-permute-start(bf16[4,24,384]{2,1,0:T(8,128)(2,1)} %get-tuple-element.34), channel_id=1, source_target_pairs={{1,0},{2,1},{3,2},{5,4},{6,5},{7,6},{9,8},{10,9},{11,10},{13,12},{... | collective-permute-start | bytes 221192 | tf_op jit(solution)/shard_map/ppermute | solution.py:373
  13.3 6.1 %collective-permute-start.3 = (bf16[2,24,384]{2,1,0:T(8,128)(2,1)}, bf16[2,24,384]{2,1,0:T(8,128)(2,1)S(1)}, u32[]{:S(2)}, u32[]{:S(2)}) collective-permute-start(bf16[2,24,384]{2,1,0:T(8,128)(2,1)} %get-tuple-element.35), channel_id=1, source_target_pairs={{0,5},{1,6},{2,7},{4,9},{5,10},{6,11},{8,13},{9,14},{10,15},{12,17... | collective-permute-start | bytes 110600 | tf_op jit(solution)/shard_map/ppermute | solution.py:376
  19.4 6.8 %collective-permute-start.4 = (bf16[2,24,384]{2,1,0:T(8,128)(2,1)}, bf16[2,24,384]{2,1,0:T(8,128)(2,1)S(1)}, u32[]{:S(2)}, u32[]{:S(2)}) collective-permute-start(bf16[2,24,384]{2,1,0:T(8,128)(2,1)} %get-tuple-element.36), channel_id=1, source_target_pairs={{1,4},{2,5},{3,6},{5,8},{6,9},{7,10},{9,12},{10,13},{11,14},{13,16... | collective-permute-start | bytes 110600 | tf_op jit(solution)/shard_map/ppermute | solution.py:377
  46.2 6.7 %collective-permute-start.6 = (f32[8,128]{1,0:T(8,128)S(1)}, f32[8,128]{1,0:T(8,128)S(1)}, u32[]{:S(2)}, u32[]{:S(2)}) collective-permute-start(f32[8,128]{1,0:T(8,128)S(1)} %add.68), channel_id=1, source_target_pairs={{0,1},{1,2},{2,3},{3,0},{4,5},{5,6},{6,7},{7,4},{8,9},{9,10},{10,1... | collective-permute-start | bytes 12296 | tf_op jit(solution)/shard_map/ppermute | solution.py:335
  47.9 5.1 %collective-permute-start.7 = (f32[8,128]{1,0:T(8,128)S(1)}, f32[8,128]{1,0:T(8,128)S(1)}, u32[]{:S(2)}, u32[]{:S(2)}) collective-permute-start(f32[8,128]{1,0:T(8,128)S(1)} %add.68), channel_id=1, source_target_pairs={{0,2},{1,3},{2,0},{3,1},{4,6},{5,7},{6,4},{7,5},{8,10},{9,11},{10,... | collective-permute-start | bytes 12296 | tf_op jit(solution)/shard_map/ppermute | solution.py:335
  52.2 4.8 %collective-permute-start.21 = (bf16[1,192,384]{2,1,0:T(8,128)(2,1)S(1)}, bf16[1,192,384]{2,1,0:T(8,128)(2,1)S(1)}, u32[]{:S(2)}, u32[]{:S(2)}) collective-permute-start(bf16[1,192,384]{2,1,0:T(8,128)(2,1)S(1)} %copy-done.31), channel_id=1, source_target_pairs={{4,12},{12,20},{20,28},{28,36},{36,44},{44,52},{52,60},{60,68},{68... | collective-permute-start | bytes 442376 | tf_op jit(solution)/shard_map/ppermute | solution.py:380
  53.9 11.0 %collective-permute-start.9 = (f32[8,128]{1,0:T(8,128)S(1)}, f32[8,128]{1,0:T(8,128)S(1)}, u32[]{:S(2)}, u32[]{:S(2)}) collective-permute-start(f32[8,128]{1,0:T(8,128)S(1)} %add_add_fusion.mid_ref), channel_id=1, source_target_pairs={{0,8},{4,12},{8,16},{12,20},{16,24},{20,28},{24,32},{28,36},{32,40... | collective-permute-start | bytes 12296 | tf_op jit(solution)/shard_map/ppermute | solution.py:332
  57.0 7.9 %collective-permute-start.10 = (f32[8,128]{1,0:T(8,128)S(1)}, f32[8,128]{1,0:T(8,128)S(1)}, u32[]{:S(2)}, u32[]{:S(2)}) collective-permute-start(f32[8,128]{1,0:T(8,128)S(1)} %add_add_fusion.mid_ref), channel_id=1, source_target_pairs={{0,248},{4,252},{8,0},{12,4},{16,8},{20,12},{24,16},{28,20},{32,24... | collective-permute-start | bytes 12296 | tf_op jit(solution)/shard_map/ppermute | solution.py:332
  60.6 50.0 %collective-permute-start.22 = (bf16[5,192,384]{2,1,0:T(8,128)(2,1)}, bf16[5,192,384]{2,1,0:T(8,128)(2,1)S(1)}, u32[]{:S(2)}, u32[]{:S(2)}) collective-permute-start(bf16[5,192,384]{2,1,0:T(8,128)(2,1)} %merge.1.a0), channel_id=1, source_target_pairs={{0,1},{1,2},{2,3},{3,0},{4,5},{5,6},{6,7},{7,4},{8,9},{9,10},{10,1... | collective-permute-start | bytes 2211848 | tf_op jit(solution)/shard_map/ppermute | solution.py:335
  60.8 50.3 %collective-permute-start.23 = (bf16[5,192,384]{2,1,0:T(8,128)(2,1)}, bf16[5,192,384]{2,1,0:T(8,128)(2,1)S(1)}, u32[]{:S(2)}, u32[]{:S(2)}) collective-permute-start(bf16[5,192,384]{2,1,0:T(8,128)(2,1)} %merge.1.a0), channel_id=1, source_target_pairs={{0,2},{1,3},{2,0},{3,1},{4,6},{5,7},{6,4},{7,5},{8,10},{9,11},{10,... | collective-permute-start | bytes 2211848 | tf_op jit(solution)/shard_map/ppermute | solution.py:335
  64.6 48.1 %collective-permute-start.24 = (bf16[5,192,384]{2,1,0:T(8,128)(2,1)}, bf16[5,192,384]{2,1,0:T(8,128)(2,1)S(1)}, u32[]{:S(2)}, u32[]{:S(2)}) collective-permute-start(bf16[5,192,384]{2,1,0:T(8,128)(2,1)} %merge.1.a0), channel_id=1, source_target_pairs={{0,3},{1,0},{2,1},{3,2},{4,7},{5,4},{6,5},{7,6},{8,11},{9,8},{10,9... | collective-permute-start | bytes 2211848 | tf_op jit(solution)/shard_map/ppermute | solution.py:335
  64.9 8.2 %collective-permute-start.11 = (f32[3,8,128]{2,1,0:T(8,128)S(1)}, f32[3,8,128]{2,1,0:T(8,128)S(1)}, u32[]{:S(2)}, u32[]{:S(2)}) collective-permute-start(f32[3,8,128]{2,1,0:T(8,128)S(1)} %pad_maximum_fusion), channel_id=1, source_target_pairs={{0,16},{4,20},{8,24},{12,28},{16,32},{20,36},{24,40},{28,44},{32,4... | collective-permute-start | bytes 36872 | tf_op jit(solution)/shard_map/ppermute | solution.py:332
  78.8 25.5 %collective-permute-start.13 = (bf16[112,768]{1,0:T(8,128)(2,1)}, bf16[112,768]{1,0:T(8,128)(2,1)S(1)}, u32[]{:S(2)}, u32[]{:S(2)}) collective-permute-start(bf16[112,768]{1,0:T(8,128)(2,1)} %get-tuple-element.42), channel_id=1, source_target_pairs={{0,1},{1,2},{2,3},{3,0},{4,5},{5,6},{6,7},{7,4},{8,9},{9,10},{10,1... | collective-permute-start | bytes 516104 | tf_op jit(solution)/shard_map/ppermute | solution.py:335
  80.8 24.2 %collective-permute-start.14 = (bf16[112,768]{1,0:T(8,128)(2,1)}, bf16[112,768]{1,0:T(8,128)(2,1)S(1)}, u32[]{:S(2)}, u32[]{:S(2)}) collective-permute-start(bf16[112,768]{1,0:T(8,128)(2,1)} %get-tuple-element.43), channel_id=1, source_target_pairs={{0,2},{1,3},{2,0},{3,1},{4,6},{5,7},{6,4},{7,5},{8,10},{9,11},{10,... | collective-permute-start | bytes 516104 | tf_op jit(solution)/shard_map/ppermute | solution.py:335
  104.3 6.3 %collective-permute-start.15 = (bf16[112,768]{1,0:T(8,128)(2,1)}, bf16[112,768]{1,0:T(8,128)(2,1)S(1)}, u32[]{:S(2)}, u32[]{:S(2)}) collective-permute-start(bf16[112,768]{1,0:T(8,128)(2,1)} %get-tuple-element.44), channel_id=1, source_target_pairs={{0,3},{1,0},{2,1},{3,2},{4,7},{5,4},{6,5},{7,6},{8,11},{9,8},{10,9... | collective-permute-start | bytes 516104 | tf_op jit(solution)/shard_map/ppermute | solution.py:335
  105.0 15.4 %collective-permute-start.16 = (bf16[112,768]{1,0:T(8,128)(2,1)}, bf16[112,768]{1,0:T(8,128)(2,1)S(1)}, u32[]{:S(2)}, u32[]{:S(2)}) collective-permute-start(bf16[112,768]{1,0:T(8,128)(2,1)} %get-tuple-element.41.a0), channel_id=1, source_target_pairs={{0,4},{4,0},{8,12},{12,8},{16,20},{20,16},{24,28},{28,24},{32,36},... | collective-permute-start | bytes 516104 | tf_op jit(solution)/shard_map/ppermute | solution.py:329
  110.6 9.8 %collective-permute-start.17 = (bf16[112,768]{1,0:T(8,128)(2,1)S(1)}, bf16[112,768]{1,0:T(8,128)(2,1)S(1)}, u32[]{:S(2)}, u32[]{:S(2)}) collective-permute-start(bf16[112,768]{1,0:T(8,128)(2,1)S(1)} %collective-permute-done.13.a1), channel_id=1, source_target_pairs={{0,4},{4,0},{8,12},{12,8},{16,20},{20,16},{24,28},{28,24},{32,36},... | collective-permute-start | bytes 516104 | tf_op jit(solution)/shard_map/ppermute | solution.py:329
  110.6 9.8 %collective-permute-start.18 = (bf16[112,768]{1,0:T(8,128)(2,1)S(1)}, bf16[112,768]{1,0:T(8,128)(2,1)S(1)}, u32[]{:S(2)}, u32[]{:S(2)}) collective-permute-start(bf16[112,768]{1,0:T(8,128)(2,1)S(1)} %collective-permute-done.14.a2), channel_id=1, source_target_pairs={{0,4},{4,0},{8,12},{12,8},{16,20},{20,16},{24,28},{28,24},{32,36},... | collective-permute-start | bytes 516104 | tf_op jit(solution)/shard_map/ppermute | solution.py:329
  111.1 9.3 %collective-permute-start.19 = (bf16[112,768]{1,0:T(8,128)(2,1)S(1)}, bf16[112,768]{1,0:T(8,128)(2,1)S(1)}, u32[]{:S(2)}, u32[]{:S(2)}) collective-permute-start(bf16[112,768]{1,0:T(8,128)(2,1)S(1)} %collective-permute-done.15.a3), channel_id=1, source_target_pairs={{0,4},{4,0},{8,12},{12,8},{16,20},{20,16},{24,28},{28,24},{32,36},... | collective-permute-start | bytes 516104 | tf_op jit(solution)/shard_map/ppermute | solution.py:329
  136.7 11.4 %collective-permute-start.25 = (bf16[3,48,896]{2,1,0:T(8,128)(2,1)}, bf16[3,48,896]{2,1,0:T(8,128)(2,1)S(1)}, u32[]{:S(2)}, u32[]{:S(2)}) collective-permute-start(bf16[3,48,896]{2,1,0:T(8,128)(2,1)} %get-tuple-element.49), channel_id=1, source_target_pairs={{0,64},{4,68},{8,72},{12,76},{16,80},{20,84},{24,88},{28,92},{32,9... | collective-permute-start | bytes 774152 | tf_op jit(solution)/shard_map/ppermute | solution.py:338
  139.7 15.1 %collective-permute-start.26 = (bf16[3,48,896]{2,1,0:T(8,128)(2,1)}, bf16[3,48,896]{2,1,0:T(8,128)(2,1)S(1)}, u32[]{:S(2)}, u32[]{:S(2)}) collective-permute-start(bf16[3,48,896]{2,1,0:T(8,128)(2,1)} %get-tuple-element.50), channel_id=1, source_target_pairs={{0,128},{4,132},{8,136},{12,140},{16,144},{20,148},{24,152},{28,15... | collective-permute-start | bytes 774152 | tf_op jit(solution)/shard_map/ppermute | solution.py:338
  142.6 12.2 %collective-permute-start.27 = (bf16[3,48,896]{2,1,0:T(8,128)(2,1)}, bf16[3,48,896]{2,1,0:T(8,128)(2,1)S(1)}, u32[]{:S(2)}, u32[]{:S(2)}) collective-permute-start(bf16[3,48,896]{2,1,0:T(8,128)(2,1)} %get-tuple-element.51), channel_id=1, source_target_pairs={{0,192},{4,196},{8,200},{12,204},{16,208},{20,212},{24,216},{28,22... | collective-permute-start | bytes 774152 | tf_op jit(solution)/shard_map/ppermute | solution.py:338
  158.1 14.1 %collective-permute-start.28 = (f32[24,896]{1,0:T(8,128)}, f32[24,896]{1,0:T(8,128)S(1)}, u32[]{:S(2)}, u32[]{:S(2)}) collective-permute-start(f32[24,896]{1,0:T(8,128)} %get-tuple-element.53), channel_id=1, source_target_pairs={{0,8},{4,12},{8,16},{12,20},{16,24},{20,28},{24,32},{28,36},{32,40... | collective-permute-start | bytes 258056 | tf_op jit(solution)/shard_map/ppermute | solution.py:341
  159.3 14.2 %collective-permute-start.29 = (f32[24,896]{1,0:T(8,128)}, f32[24,896]{1,0:T(8,128)S(1)}, u32[]{:S(2)}, u32[]{:S(2)}) collective-permute-start(f32[24,896]{1,0:T(8,128)} %get-tuple-element.54), channel_id=1, source_target_pairs={{0,16},{4,20},{8,24},{12,28},{16,32},{20,36},{24,40},{28,44},{32,4... | collective-permute-start | bytes 258056 | tf_op jit(solution)/shard_map/ppermute | solution.py:341
  164.9 13.1 %collective-permute-start.30 = (f32[24,896]{1,0:T(8,128)}, f32[24,896]{1,0:T(8,128)S(1)}, u32[]{:S(2)}, u32[]{:S(2)}) collective-permute-start(f32[24,896]{1,0:T(8,128)} %get-tuple-element.55), channel_id=1, source_target_pairs={{0,24},{4,28},{8,32},{12,36},{16,40},{20,44},{24,48},{28,52},{32,5... | collective-permute-start | bytes 258056 | tf_op jit(solution)/shard_map/ppermute | solution.py:341
  164.9 13.2 %collective-permute-start.31 = (f32[24,896]{1,0:T(8,128)}, f32[24,896]{1,0:T(8,128)S(1)}, u32[]{:S(2)}, u32[]{:S(2)}) collective-permute-start(f32[24,896]{1,0:T(8,128)} %get-tuple-element.56), channel_id=1, source_target_pairs={{0,32},{4,36},{8,40},{12,44},{16,48},{20,52},{24,56},{28,60},{32,0... | collective-permute-start | bytes 258056 | tf_op jit(solution)/shard_map/ppermute | solution.py:341
  168.2 13.6 %collective-permute-start.32 = (f32[24,896]{1,0:T(8,128)}, f32[24,896]{1,0:T(8,128)S(1)}, u32[]{:S(2)}, u32[]{:S(2)}) collective-permute-start(f32[24,896]{1,0:T(8,128)} %get-tuple-element.57), channel_id=1, source_target_pairs={{0,40},{4,44},{8,48},{12,52},{16,56},{20,60},{24,0},{28,4},{32,8},... | collective-permute-start | bytes 258056 | tf_op jit(solution)/shard_map/ppermute | solution.py:341
  172.2 12.2 %collective-permute-start.33 = (f32[24,896]{1,0:T(8,128)}, f32[24,896]{1,0:T(8,128)S(1)}, u32[]{:S(2)}, u32[]{:S(2)}) collective-permute-start(f32[24,896]{1,0:T(8,128)} %get-tuple-element.58), channel_id=1, source_target_pairs={{0,48},{4,52},{8,56},{12,60},{16,0},{20,4},{24,8},{28,12},{32,16},... | collective-permute-start | bytes 258056 | tf_op jit(solution)/shard_map/ppermute | solution.py:341
  173.5 11.9 %collective-permute-start.34 = (f32[24,896]{1,0:T(8,128)}, f32[24,896]{1,0:T(8,128)S(1)}, u32[]{:S(2)}, u32[]{:S(2)}) collective-permute-start(f32[24,896]{1,0:T(8,128)} %get-tuple-element.59), channel_id=1, source_target_pairs={{0,56},{4,60},{8,0},{12,4},{16,8},{20,12},{24,16},{28,20},{32,24},... | collective-permute-start | bytes 258056 | tf_op jit(solution)/shard_map/ppermute | solution.py:341
  (35 other events, 234.2 us)

commit v2 on v1

v2 whole, which is shorter than its diff:
```python
import functools

import jax
import jax.numpy as jnp
import numpy as np
from jax import lax
from jax.experimental import pallas as pl
from jax.experimental.pallas import tpu as pltpu
from jax.sharding import PartitionSpec as P

F32 = jnp.float32
B16 = jnp.bfloat16
COLS = 24
LIMIT = 56 * 1024 * 1024
NT = (((1,), (1,)), ((), ()))
TN = (((0,), (0,)), ((), ()))


def dot(a, b, dims=None):
    if dims is None:
        return jnp.dot(a, b, preferred_element_type=F32)
    return lax.dot_general(a, b, dims, preferred_element_type=F32)


def call(kernel, outs, scratch=(), **kw):
    params = pltpu.CompilerParams(vmem_limit_bytes=LIMIT)
    return pl.pallas_call(kernel, out_shape=outs, scratch_shapes=list(scratch), compiler_params=params, **kw)


def smem():
    return pl.BlockSpec(memory_space=pltpu.SMEM)


def vmem():
    return pl.BlockSpec(memory_space=pltpu.VMEM)


def half_table(chans, run, ny, nz):
    lane = np.arange(chans // 2)
    block = wide(run) * nz
    place = (lane // run // nz) * block + (lane % run) * nz + lane // run % nz
    table = np.zeros((2, chans, ny * block), np.float32)
    for core in range(2):
        table[core, (lane // run) * 2 * run + core * run + lane % run, place] = 1
    return table


def wide(run):
    return -(-run // 8) * 8


def first_kernel(x_ref, past_ref, last_ref, top_ref, bot_ref, ptop_ref, pbot_ref):
    nf, band, chans = x_ref.shape
    past_ref[...] = x_ref[nf - 2 :]
    last_ref[0] = x_ref[nf - 1]
    for f in range(nf):
        wide_frame = x_ref[f].astype(F32)
        top = wide_frame[:COLS].astype(B16)
        bot = wide_frame[band - COLS :].astype(B16)
        top_ref[f] = top
        bot_ref[f] = bot
        if f >= nf - 2:
            ptop_ref[f - nf + 2] = top
            pbot_ref[f - nf + 2] = bot


def choose_kernel(at_ref, frames_ref, p0, p1, p2, p3, table_ref, own_ref, oth_ref):
    c = at_ref[0]
    band = frames_ref.shape[2]

    @pl.when(pl.program_id(0) == 0)
    def _():
        for d, ref in enumerate((p0, p1, p2, p3)):
            at = pl.ds(pl.multiple_of(lax.rem(at_ref[1] - d + 4, 4) * band, band), band)
            own_ref[0, at] = dot(ref[0], table_ref[c]).astype(B16)
            oth_ref[0, at] = dot(ref[0], table_ref[1 - c]).astype(B16)

    @pl.when(pl.program_id(0) > 0)
    def _():
        for xs in range(4):
            at = slice(xs * band, (xs + 1) * band)
            own_ref[0, at] = dot(frames_ref[xs, 0], table_ref[c]).astype(B16)
            oth_ref[0, at] = dot(frames_ref[xs, 0], table_ref[1 - c]).astype(B16)


def forward_kernel(at_ref, pos_ref, x_ref, past_ref, top_ref, bot_ref, ptop_ref, pbot_ref, w_ref, hw_ref,
                   lat_ref, kf_ref, d0, d1, d2, d3, pre_ref, wide_ref, turned_ref, head_ref):
    step = pl.program_id(0)
    nf, band, chans = x_ref.shape
    rows = band + 2 * COLS

    @pl.when(step == 0)
    def _():
        col = lax.rem(lax.broadcasted_iota(jnp.int32, (rows, 1), 0), COLS)
        for f in range(nf + 2):
            if f < 2:
                parts = (ptop_ref[f], past_ref[f], pbot_ref[f])
            else:
                parts = (top_ref[f - 2], x_ref[f - 2], bot_ref[f - 2])
            v = jnp.concatenate([p.astype(F32) for p in parts], axis=0)
            for dw in range(3):
                if dw == 0:
                    s = jnp.where(col > 0, pltpu.roll(v, 1, 0), 0.0)
                elif dw == 2:
                    s = jnp.where(col < COLS - 1, pltpu.roll(v, rows - 1, 0), 0.0)
                else:
                    s = v
                for dh in range(3):
                    wide_ref[dh, f * band : (f + 1) * band, dw * chans : (dw + 1) * chans] = s[
                        dh * COLS : dh * COLS + band
                    ].astype(B16)

    dt, dh = step // 3, lax.rem(step, 3)
    part = dot(wide_ref[dh, pl.ds(pl.multiple_of(dt * band, band), nf * band), :], w_ref[0])
    for f in range(nf):
        keep = jnp.where(pos_ref[f] >= 2 - dt, 1.0, 0.0)
        piece = keep * part[f * band : (f + 1) * band]

        @pl.when(step == 0)
        def _():
            pre_ref[f * band : (f + 1) * band] = piece

        @pl.when(step > 0)
        def _():
            pre_ref[f * band : (f + 1) * band] += piece

    @pl.when(step == 8)
    def _():
        zdim = lat_ref.shape[1] // 2
        row = lax.broadcasted_iota(jnp.int32, kf_ref.shape, 0)
        kf = jnp.zeros(kf_ref.shape, F32)
        for f in range(nf):
            at = slice(f * band, (f + 1) * band)
            pre = pre_ref[at]
            sig = 1.0 / (1.0 + jnp.exp(-pre))
            act = (pre * sig).astype(B16)
            lat = dot(act, hw_ref[...])
            lat_ref[at] = lat
            lane = lax.broadcasted_iota(jnp.int32, lat.shape, 1)
            grow = jnp.exp(lat) - 1.0
            term = jnp.where(lane < zdim, lat * lat, grow - lat)
            kf = jnp.where(row == at_ref[0] * nf + f, 0.5 * jnp.sum(term), kf)
            dlat = jnp.where(lane < zdim, lat, 0.5 * grow).astype(B16)
            dact = dot(dlat, hw_ref[...], NT)
            pre_ref[at] = (dact * sig * (1.0 + pre * (1.0 - sig))).astype(B16).astype(F32)
            head_ref[f] = dot(dlat, act, TN)
        kf_ref[...] = kf
        turned_ref[...] = jnp.transpose(pre_ref[...], (1, 0)).astype(B16)
        block = chans // 4
        hblock = 2 * zdim // 4
        for d, ref in enumerate((d0, d1, d2, d3)):
            to = lax.rem(at_ref[1] + d, 4)
            ref[:block] = turned_ref[pl.ds(pl.multiple_of(to * block, block), block), :]
            heads = [head_ref[f, pl.ds(pl.multiple_of(to * hblock, hblock), hblock), :] for f in range(nf)]
            pad = ref.shape[1] - 2 * chans
            if pad:
                heads = [jnp.concatenate([h, jnp.zeros((hblock, pad // 2), F32)], axis=1) for h in heads]
            both = jnp.concatenate(
                [jnp.concatenate(heads[:2], axis=1), jnp.concatenate(heads[2:], axis=1)], axis=0
            )
            ref[block:] = both.astype(B16)


def weight_kernel(ny, at_ref, keep_ref, g_ref, loss_ref, a0, a1, a2, a3, b0, b1, b2, b3, x_ref, xo_ref, direct_ref,
                  *refs):
    sends, (held_ref, taps_ref, acc_ref, out_ref, xs_ref, sem) = refs[:ny], refs[ny:]
    c, x, y = at_ref[0], at_ref[1], at_ref[2]
    copies = []
    for core, ref, s in ((c, x_ref, 0), (1 - c, xo_ref, 1)):
        copies.append(pltpu.make_async_copy(ref.at[0:1], xs_ref.at[pl.ds(core, 1)], sem.at[s, 0]))
        copies.append(pltpu.make_async_copy(ref.at[1:5], xs_ref.at[pl.ds(2 + 4 * core, 4)], sem.at[s, 1]))
    for copy in copies:
        copy.start()
    full = x_ref.shape[1]
    band = full // 4
    block = taps_ref.shape[0] // 9
    chans = direct_ref.shape[1]
    lanes = acc_ref.shape[2]
    hblock = (held_ref.shape[2] - block) // 2
    half = full // 2
    hsum = jnp.zeros((hblock, chans), F32)
    for core, given in ((c, (a0, a1, a2, a3)), (1 - c, (b0, b1, b2, b3))):
        for d, ref in enumerate(given):
            held_ref[core, lax.rem(x - d + 4, 4)] = ref[...]
            tail = ref[block:, :].astype(F32)
            for f in range(4):
                part = tail[(f // 2) * hblock : (f // 2 + 1) * hblock, (f % 2) * half : (f % 2) * half + chans]
                hsum = hsum + g_ref[core * 4 + f] * part
    acc_ref[...] = jnp.zeros(acc_ref.shape, F32)
    lane = lax.broadcasted_iota(jnp.int32, (1, full), 1)
    col = lax.rem(lane, COLS)
    line = lane // COLS

    for copy in copies:
        copy.wait()

    def core_frames(core, carry):
        for lf in range(4):
            frame = jnp.zeros((block, full), F32)
            for xs in range(4):
                v = held_ref[core, xs, :block, :].astype(F32)
                shift = ((xs - lf) * band) % full
                if shift:
                    v = pltpu.roll(v, shift, 1)
                frame = jnp.where(lane // band == xs, v, frame)
            for dw in range(3):
                if dw == 0:
                    v = jnp.where(col < COLS - 1, pltpu.roll(frame, full - 1, 1), 0.0)
                elif dw == 2:
                    v = jnp.where(col > 0, pltpu.roll(frame, 1, 1), 0.0)
                else:
                    v = frame
                for dh in range(3):
                    if dh == 0:
                        s = jnp.where(line < full // COLS - 1, pltpu.roll(v, full - COLS, 1), 0.0)
                    elif dh == 2:
                        s = jnp.where(line > 0, pltpu.roll(v, COLS, 1), 0.0)
                    else:
                        s = v
                    q = dh * 3 + dw
                    taps_ref[q * block : (q + 1) * block, :] = s.astype(B16)
            f = core * 4 + lf
            for dt in range(3):
                acc_ref[dt, : 9 * block] += keep_ref[f * 3 + dt] * dot(taps_ref[...], xs_ref[f + dt])
        return carry

    lax.fori_loop(0, 2, core_frames, 0)
    direct = direct_ref[c]
    high = hsum.astype(B16)
    low = (hsum - high.astype(F32)).astype(B16)
    acc_ref[0, 9 * block : 9 * block + hblock] = dot(high, direct) + dot(low, direct)
    loss = jnp.full((8, lanes), loss_ref[0], F32)
    top = loss.astype(B16).astype(F32)
    mid = (loss - top).astype(B16).astype(F32)
    acc_ref[1, 9 * block : 9 * block + 8] = top
    acc_ref[1, 9 * block + 8 : 9 * block + 16] = mid
    acc_ref[1, 9 * block + 16 : 9 * block + 24] = loss - top - mid
    rows = sends[0].shape[1]
    ystep = lanes // ny
    for dt in range(3):
        out_ref[...] = jnp.transpose(acc_ref[dt], (1, 0))
        for d, ref in enumerate(sends):
            to = lax.rem(y + d, ny)
            ref[dt] = out_ref[pl.ds(pl.multiple_of(to * ystep, 8), rows), :].astype(ref.dtype)


def add_kernel(ny, nz, run, at_ref, *refs):
    gets, sends, (sum_ref, part_ref) = refs[:ny], refs[ny : ny + nz], refs[ny + nz :]
    total = gets[0][...]
    for ref in gets[1:]:
        total = total + ref[...].astype(F32)
    chunk = sum_ref.shape[3]
    for i in range(sum_ref.shape[0]):
        sum_ref[i] = total[:, :, i * chunk : (i + 1) * chunk]
    part_ref[...] = jnp.zeros(part_ref.shape, F32)
    step = part_ref.shape[1] // 3
    for z in range(nz):
        for dt in range(3):
            for i in range(sum_ref.shape[0]):
                part_ref[z, dt * step : dt * step + run, i * chunk : (i + 1) * chunk] = sum_ref[
                    i, dt, pl.ds(z, run, stride=nz), :
                ]
    for d, ref in enumerate(sends):
        ref[...] = part_ref[lax.rem(at_ref[3] + d, nz)].astype(ref.dtype)


def last_kernel(count, *refs):
    parts, (weight_ref, head_ref, loss_ref) = refs[:count], refs[count:]
    total = parts[0][...]
    for ref in parts[1:]:
        total = total + ref[...].astype(F32)
    run, block = weight_ref.shape[1:]
    step = total.shape[0] // 3
    for dt in range(3):
        for q in range(9):
            weight_ref[dt * 9 + q] = total[dt * step : dt * step + run, q * block : (q + 1) * block]
    base = 9 * block
    head_ref[...] = total[:run, base : base + head_ref.shape[1]]
    loss = total[step : step + 1, base : base + 1]
    loss = loss + total[step : step + 1, base + 8 : base + 9]
    loss_ref[...] = loss + total[step : step + 1, base + 16 : base + 17]


def body(frames, conv_weight, head_weight, clip_len):
    nf, nrow, ncol, chans = frames.shape
    band = nrow * ncol
    cells = nf * band
    count = lax.axis_size("tm")
    ny = 4 if count == 64 else 2
    nz = count // 2 // ny
    run = chans // count
    chip = 2 * nf
    t, x = lax.axis_index("tm"), lax.axis_index("space")
    c, k = t % 2, t // 2
    y, z = k // nz, k % nz
    at = jnp.stack([c, x, y, z]).astype(jnp.int32)
    shape = jax.ShapeDtypeStruct

    def index(yy, zz, cc):
        return ((yy % ny) * nz + zz % nz) * 2 + cc

    every = [(yy, zz, cc) for yy in range(ny) for zz in range(nz) for cc in range(2)]

    def over_core(v):
        return lax.ppermute(v, "tm", [(i, i ^ 1) for i in range(count)])

    def over_chip(v, d):
        return lax.ppermute(v, "tm", [(i, (i + 2 * d) % count) for i in range(count)])

    def over_x(v, d):
        return lax.ppermute(v, "space", [(i, (i + d) % 4) for i in range(4)])

    def over_y(v, d):
        return lax.ppermute(v, "tm", [(index(a, b, e), index(a + d, b, e)) for a, b, e in every])

    def over_z(v, d):
        return lax.ppermute(v, "tm", [(index(a, b, e), index(a, b + d, e)) for a, b, e in every])

    nclip = clip_len.shape[0]
    order = jnp.arange(nclip)
    ends = jnp.sum(jnp.where(order[None, :] <= order[:, None], clip_len[None, :], 0), axis=1)
    ids = chip * k + jnp.arange(-3 * chip, 4 * chip)
    clip = jnp.where(ids < 0, -1, jnp.sum(ends[None, :] <= ids[:, None], axis=1))
    mine = clip[3 * chip : 4 * chip]
    same = (clip[:, None] == mine[None, :]).astype(F32)
    member = mine[:, None] == order[None, :]
    lens = jnp.sum(jnp.where(member, clip_len[None, :], 0), axis=1)
    pos = ids[3 * chip : 4 * chip] - jnp.sum(jnp.where(member, (ends - clip_len)[None, :], 0), axis=1)
    lens = lens.astype(F32)
    keep = (pos[:, None] >= jnp.array([2, 1, 0])[None, :]).astype(F32).reshape(-1)
    own_pos = lax.dynamic_slice_in_dim(pos, c * nf, nf).astype(jnp.int32)

    table = jnp.asarray(half_table(chans, run, ny, nz), B16)
    flat = frames.reshape(nf, band, chans)
    gathered = lax.all_gather(flat, "space", axis=0)
    past, last, top, bot, ptop, pbot = call(
        first_kernel,
        [shape((2, band, chans), B16), shape((1, band, chans), B16)]
        + [shape((nf, ncol, chans), B16)] * 2
        + [shape((2, ncol, chans), B16)] * 2,
        name="first",
    )(flat)
    both = ("tm", "space")
    top, bot = (
        lax.ppermute(bot, "space", [(i, i + 1) for i in range(3)]),
        lax.ppermute(top, "space", [(i + 1, i) for i in range(3)]),
    )
    past = lax.ppermute(past, "tm", [(i, i + 1) for i in range(count - 1)])
    ptop, pbot = (
        lax.ppermute(pbot, both, [(4 * i + j, 4 * (i + 1) + j + 1) for i in range(count - 1) for j in range(3)]),
        lax.ppermute(ptop, both, [(4 * i + j + 1, 4 * (i + 1) + j) for i in range(count - 1) for j in range(3)]),
    )
    last = lax.ppermute(last, "tm", [(i, i + 2) for i in range(1, count - 2, 2)])
    before = jnp.where(c == 0, past[:1], last)
    before, flat = lax.optimization_barrier((before, flat))
    befores = [before] + [over_x(before, d) for d in (1, 2, 3)]

    whole = lambda *dims: pl.BlockSpec(dims, lambda i: (0,) * len(dims))
    zlat = head_weight.shape[1]
    hblock = zlat // 4
    block = chans // 4
    message = shape((block + 2 * hblock, cells), B16)
    latent, kframe, *mine_d = call(
        forward_kernel,
        [shape((cells, zlat), F32), shape((chip, 128), F32)] + [message] * 4,
        [
            pltpu.VMEM((cells, chans), F32),
            pltpu.VMEM((3, (nf + 2) * band, 3 * chans), B16),
            pltpu.VMEM((chans, cells), B16),
            pltpu.VMEM((nf, zlat, chans), F32),
        ],
        grid=(9,),
        in_specs=[smem(), smem()]
        + [whole(*v.shape) for v in (flat, past, top, bot, ptop, pbot)]
        + [pl.BlockSpec((1, 3 * chans, chans), lambda i: (i, 0, 0)), whole(chans, zlat)],
        out_specs=[whole(cells, zlat), whole(chip, 128)] + [whole(*message.shape)] * 4,
        name="forward",
    )(at, own_pos, flat, past, top, bot, ptop, pbot, conv_weight.reshape(9, 3 * chans, chans), head_weight)
    mine_d = [mine_d[0]] + [over_x(mine_d[d], d) for d in (1, 2, 3)]

    kchip = kframe + over_core(kframe)
    gathered, befores, kchip = lax.optimization_barrier((gathered, befores, kchip))
    kchip, mine_d = lax.optimization_barrier((kchip, mine_d))
    kchip = kchip + over_x(kchip, 1) + over_x(kchip, 2) + over_x(kchip, 3)
    core_d = [over_core(v) for v in mine_d]
    triple = jnp.stack([over_chip(kchip, 1), kchip, over_chip(kchip, -1)])
    left, right = over_chip(triple, 2), over_chip(triple, -2)
    window = jnp.concatenate([left, kchip[None], right])[:, :, 0].reshape(-1)
    per_frame = float(4 * band)
    totals = jnp.sum(same * window[:, None], axis=0)
    gain = lens / (lens * per_frame + totals)
    first = (pos == 0).astype(F32)
    loss_part = jnp.sum(first * lens * jnp.log1p(totals / (lens * per_frame)))
    scale = (keep.reshape(chip, 3) * gain[:, None]).reshape(-1)

    lanes = table.shape[2]
    chosen = shape((5, 4 * band, lanes), B16)
    spec = pl.BlockSpec((1, 4 * band, lanes), lambda i: (i, 0, 0))
    xown, xoth = call(
        choose_kernel,
        [chosen, chosen],
        grid=(5,),
        in_specs=[
            smem(),
            pl.BlockSpec((4, 1, band, chans), lambda i: (0, jnp.maximum(i - 1, 0), 0, 0)),
        ]
        + [whole(1, band, chans)] * 4
        + [
            whole(*table.shape),
        ],
        out_specs=[spec, spec],
        name="choose",
    )(at, gathered, *befores, table)
    xoth = over_core(xoth)

    rows = run * nz
    wrow = 9 * block + 32
    sends = call(
        functools.partial(weight_kernel, ny),
        [shape((3, rows, wrow), F32)] + [shape((3, rows, wrow), B16)] * (ny - 1),
        [
            pltpu.VMEM((2, 4) + message.shape, B16),
            pltpu.VMEM((9 * block, 4 * band), B16),
            pltpu.VMEM((3, wrow, lanes), F32),
            pltpu.VMEM((lanes, wrow), F32),
            pltpu.VMEM((10, 4 * band, lanes), B16),
            pltpu.SemaphoreType.DMA((2, 2)),
        ],
        in_specs=[smem()] * 4 + [vmem()] * 8 + [pl.BlockSpec(memory_space=pl.ANY)] * 2 + [vmem()],
        name="weight",
    )(at, scale, gain, loss_part[None], *mine_d, *core_d, xown, xoth, table)
    gets = [sends[0]] + [over_y(sends[d], d) for d in range(1, ny)]
    step = wide(run)
    chunk = 128 if wrow % 128 == 0 else wrow
    parts = call(
        functools.partial(add_kernel, ny, nz, run),
        [shape((3 * step, wrow), F32)] + [shape((3 * step, wrow), B16)] * (nz - 1),
        [pltpu.VMEM((wrow // chunk, 3, rows, chunk), F32), pltpu.VMEM((nz, 3 * step, wrow), F32)],
        in_specs=[smem()] + [vmem()] * ny,
        name="add",
    )(at, *gets)
    parts = [parts[0]] + [over_z(parts[d], d) for d in range(1, nz)]
    weight_grad, head_grad, loss = call(
        functools.partial(last_kernel, nz),
        [shape((27, run, block), F32), shape((run, hblock), F32), shape((1, 1), F32)],
        name="last",
    )(*parts)
    return latent.reshape(nf, nrow, ncol, zlat), loss[0, 0], weight_grad, head_grad


def solution(mesh):
    in_specs = (P("tm", "space", None, None), P(), P(), P())
    out_specs = (P("tm", "space", None, None), P(), P(None, "tm", "space"), P("tm", "space"))
    return jax.shard_map(body, mesh=mesh, in_specs=in_specs, out_specs=out_specs, check_vma=False)
```

time: 196 us -> 180 us (0.918)
  waiting for transfers between devices: 59.6 us -> 36.3 us
  between operations: 4.09 us -> 14.5 us
  starting transfers between devices: 60.9 us -> 67.5 us
  Pallas kernels: 52.3 us -> 45.9 us
  local copies, waits for them, and re-layouts: 13.2 us -> 8.56 us
    ppermute x9, waiting for transfers between devices: 30.1 us -> 7.98 us  [over_x(): return lax.ppermute(v, 'space', [(i, (i + d) % 4) for i in range(4)])]
    pallas_call x6 -> x4, Pallas kernels: 34.4 us -> 27.2 us  [the longest x1 16.8 us: body(): call(forward_kernel, [shape((cells, zlat), F32), shape((chip, 128), F32)]...]
    ppermute x7, waiting for transfers between devices: 11.5 us -> 4.43 us  [over_z(): lax.ppermute(v, 'tm', [(index(a, b, e), index(a, b + d, e)) for a, b, e i...]
    ppermute x1, waiting for transfers between devices: 0.01 us -> 6.1 us  [body(): lax.ppermute(bot, 'space', [(i, i + 1) for i in range(3)])]
    ppermute x9, starting transfers between devices: 12.3 us -> 17.8 us  [over_x(): return lax.ppermute(v, 'space', [(i, (i + d) % 4) for i in range(4)])]
    ppermute x1, starting transfers between devices: 3.62 us -> 7.9 us  [body(): lax.ppermute(pbot, both, [(4 * i + j, 4 * (i + 1) + j + 1) for i in range...]
    ppermute x1, waiting for transfers between devices: 3.36 us -> 0.01 us  [body(): lax.ppermute(ptop, both, [(4 * i + j + 1, 4 * (i + 1) + j) for i in range...]
    slice x2 -> x0, local copies, waits for them, and re-layouts: 2.25 us -> none  [the longest x1 1.43 us: body(): loss = total[1, 0, base] + total[1, 0, base + 8] + total[1, 0, base + 16]]
  transfers between devices with their start and end apart: 35 -> 36, of which waited for: 15 -> 17; matrix products, arithmetic and copies ran while one was open for 4% -> 4% of each run, Pallas kernels for 15% -> 11%
where the time goes in v2:
time: 180 us; the launch traced here: 178 us
  starting transfers between devices  67.5 us (38%)
  Pallas kernels  45.9 us (26%)
  waiting for transfers between devices  36.3 us (20%)
  between operations  14.5 us (8%)
  local copies, waits for them, and re-layouts  8.56 us (5%)
  other arithmetic  4.78 us (3%)
    ppermute x9, starting transfers between devices, over_x(): return lax.ppermute(v, 'space', [(i, (i + d) % 4) for i in range(4)])  17.8 us
    pallas_call x1, Pallas kernels, body(): call(forward_kernel, [shape((cells, zlat), F32), shape((chip, 128), F32)]...  16.8 us
    ppermute x7, starting transfers between devices, over_z(): lax.ppermute(v, 'tm', [(index(a, b, e), index(a, b + d, e)) for a, b, e i...  16.5 us
    pallas_call x1, Pallas kernels, body(): call(functools.partial(weight_kernel, ny), [shape((3, rows, wrow), F32)]...  16.2 us
    ppermute x3, waiting for transfers between devices, over_y(): lax.ppermute(v, 'tm', [(index(a, b, e), index(a + d, b, e)) for a, b, e i...  11 us
    ppermute x4, starting transfers between devices, over_chip(): lax.ppermute(v, 'tm', [(i, (i + 2 * d) % count) for i in range(count)])  8.27 us
    ppermute x9, waiting for transfers between devices, over_x(): return lax.ppermute(v, 'space', [(i, (i + d) % 4) for i in range(4)])  7.98 us
    ppermute x1, starting transfers between devices, body(): lax.ppermute(pbot, both, [(4 * i + j, 4 * (i + 1) + j + 1) for i in range...  7.9 us
  transfers between devices with their start and end apart: 36, of which 17 were waited for; matrix products, arithmetic and copies ran while one was open for 4% of the time, Pallas kernels for 11%

profile of v2, /device:TPU:32, one launch (start us, length us, event | category | flops | bytes accessed | tf_op | source)
XLA Modules:
  0.0 177.5 jit_solution(11731999447157368216)
XLA Ops:
  7.9 1.9 %first.1 = (bf16[2,192,384]{2,1,0:T(8,128)(2,1)}, bf16[1,192,384]{2,1,0:T(8,128)(2,1)}, bf16[4,24,384]{2,1,0:T(8,128)(2,1)}, bf16[4,24,384]{2,1,0:T(8,128)(2,1)}...) custom-call(bf16[4,192,384]{2,1,0:T(8,128)(2,1)} %bitcast.15), custom_call_target="tpu_custom_call" | custom-call | tf_op jit(solution)/shard_map/first/pallas_call | solution.py:336
  9.8 1.9 %collective-permute-start = (bf16[2,192,384]{2,1,0:T(8,128)(2,1)}, bf16[2,192,384]{2,1,0:T(8,128)(2,1)S(1)}, u32[]{:S(2)}, u32[]{:S(2)}) collective-permute-start(bf16[2,192,384]{2,1,0:T(8,128)(2,1)} %get-tuple-element.46), channel_id=1, source_target_pairs={{0,4},{4,8},{8,12},{12,16},{16,20},{20,24},{24,28},{28,32},{32,36}... | collective-permute-start | bytes 884744 | tf_op jit(solution)/shard_map/ppermute | solution.py:348
  12.4 7.9 %collective-permute-start.4 = (bf16[2,24,384]{2,1,0:T(8,128)(2,1)}, bf16[2,24,384]{2,1,0:T(8,128)(2,1)S(1)}, u32[]{:S(2)}, u32[]{:S(2)}) collective-permute-start(bf16[2,24,384]{2,1,0:T(8,128)(2,1)} %get-tuple-element.51), channel_id=1, source_target_pairs={{0,5},{1,6},{2,7},{4,9},{5,10},{6,11},{8,13},{9,14},{10,15},{12,17... | collective-permute-start | bytes 110600 | tf_op jit(solution)/shard_map/ppermute | solution.py:350
  24.2 2.2 %collective-permute-start.6 = (bf16[1,192,384]{2,1,0:T(8,128)(2,1)S(1)}, bf16[1,192,384]{2,1,0:T(8,128)(2,1)S(1)}, u32[]{:S(2)}, u32[]{:S(2)}) collective-permute-start(bf16[1,192,384]{2,1,0:T(8,128)(2,1)S(1)} %slice_select_fusion.p0), channel_id=1, source_target_pairs={{0,1},{1,2},{2,3},{3,0},{4,5},{5,6},{6,7},{7,4},{8,9},{9,10},{10,1... | collective-permute-start | bytes 442376 | tf_op jit(solution)/shard_map/ppermute | solution.py:311
  26.4 2.1 %collective-permute-start.7 = (bf16[1,192,384]{2,1,0:T(8,128)(2,1)S(1)}, bf16[1,192,384]{2,1,0:T(8,128)(2,1)S(1)}, u32[]{:S(2)}, u32[]{:S(2)}) collective-permute-start(bf16[1,192,384]{2,1,0:T(8,128)(2,1)S(1)} %slice_select_fusion.p0), channel_id=1, source_target_pairs={{0,2},{1,3},{2,0},{3,1},{4,6},{5,7},{6,4},{7,5},{8,10},{9,11},{10,... | collective-permute-start | bytes 442376 | tf_op jit(solution)/shard_map/ppermute | solution.py:311
  28.5 1.8 %collective-permute-start.8 = (bf16[1,192,384]{2,1,0:T(8,128)(2,1)S(1)}, bf16[1,192,384]{2,1,0:T(8,128)(2,1)S(1)}, u32[]{:S(2)}, u32[]{:S(2)}) collective-permute-start(bf16[1,192,384]{2,1,0:T(8,128)(2,1)S(1)} %slice_select_fusion.p0), channel_id=1, source_target_pairs={{0,3},{1,0},{2,1},{3,2},{4,7},{5,4},{6,5},{7,6},{8,11},{9,8},{10,9... | collective-permute-start | bytes 442376 | tf_op jit(solution)/shard_map/ppermute | solution.py:311
  32.4 2.1 %collective-permute-start.2 = (bf16[4,24,384]{2,1,0:T(8,128)(2,1)}, bf16[4,24,384]{2,1,0:T(8,128)(2,1)S(1)}, u32[]{:S(2)}, u32[]{:S(2)}) collective-permute-start(bf16[4,24,384]{2,1,0:T(8,128)(2,1)} %get-tuple-element.49), channel_id=1, source_target_pairs={{0,1},{1,2},{2,3},{4,5},{5,6},{6,7},{8,9},{9,10},{10,11},{12,13},{... | collective-permute-start | bytes 221192 | tf_op jit(solution)/shard_map/ppermute | solution.py:345
  36.5 6.1 %collective-permute-done.2.top_ref = bf16[4,24,384]{2,1,0:T(8,128)(2,1)S(1)} collective-permute-done((bf16[4,24,384]{2,1,0:T(8,128)(2,1)}, bf16[4,24,384]{2,1,0:T(8,128)(2,1)S(1)}, u32[]{:S(2)}, u32[]{:S(2)}) %collective-permute-start.2) | collective-permute-done | bytes 73760 | tf_op jit(solution)/shard_map/ppermute | solution.py:345
  42.6 2.2 %collective-permute-done.3.bot_ref = bf16[4,24,384]{2,1,0:T(8,128)(2,1)S(1)} collective-permute-done((bf16[4,24,384]{2,1,0:T(8,128)(2,1)}, bf16[4,24,384]{2,1,0:T(8,128)(2,1)S(1)}, u32[]{:S(2)}, u32[]{:S(2)}) %collective-permute-start.3) | collective-permute-done | bytes 73760 | tf_op jit(solution)/shard_map/ppermute | solution.py:346
  45.5 16.8 %forward.1 = (f32[768,32]{1,0:T(8,128)}, f32[8,128]{1,0:T(8,128)}, bf16[112,768]{1,0:T(8,128)(2,1)}, bf16[112,768]{1,0:T(8,128)(2,1)}, bf16[112,768]{1,0:T(8,128)(2,1)}, /*index=5*/bf16[112,768]{1,0:T(8,128)(2,1)}) custom-call(s32[4]{0:T(128)} %pad_add_fusion.at_ref, s32[4]{0:T(128)} %dynamic_slice.3.pos_ref, bf16[4,192,384]{2,1,0:T(8,128)(2,1)} %bitcast.16, ...), custom_call_target="tpu_custom_call" | custom-call | tf_op jit(solution)/shard_map/forward/pallas_call | solution.py:363
  62.4 2.8 %collective-permute-start.9 = (f32[8,128]{1,0:T(8,128)}, f32[8,128]{1,0:T(8,128)S(1)}, u32[]{:S(2)}, u32[]{:S(2)}) collective-permute-start(f32[8,128]{1,0:T(8,128)} %get-tuple-element.55), channel_id=1, source_target_pairs={{0,4},{4,0},{8,12},{12,8},{16,20},{20,16},{24,28},{28,24},{32,36},... | collective-permute-start | bytes 12296 | tf_op jit(solution)/shard_map/ppermute | solution.py:305
  67.7 6.8 %choose.1 = (bf16[5,768,256]{2,1,0:T(8,128)(2,1)}, bf16[5,768,256]{2,1,0:T(8,128)(2,1)}) custom-call(s32[4]{0:T(128)} %pad_add_fusion.at_ref, bf16[4,4,192,384]{3,2,1,0:T(8,128)(2,1)} %all-gather.2.cloned.1.call-done.frames_ref, bf16[1,192,384]{2,1,0:T(8,128)(2,1)} %copy-done.2, bf16[1,192,384]{2,1,0:T(8,128)(2,1)} %copy-done.14, ...), custom_call_target="tpu_custom_call" | custom-call | tf_op jit(solution)/shard_map/choose/pallas_call | solution.py:399
  74.8 3.3 %collective-permute-start.11 = (bf16[112,768]{1,0:T(8,128)(2,1)S(1)}, bf16[112,768]{1,0:T(8,128)(2,1)S(1)}, u32[]{:S(2)}, u32[]{:S(2)}) collective-permute-start(bf16[112,768]{1,0:T(8,128)(2,1)S(1)} %copy-done.31), channel_id=1, source_target_pairs={{0,2},{1,3},{2,0},{3,1},{4,6},{5,7},{6,4},{7,5},{8,10},{9,11},{10,... | collective-permute-start | bytes 516104 | tf_op jit(solution)/shard_map/ppermute | solution.py:311
  78.1 2.5 %collective-permute-start.12 = (bf16[112,768]{1,0:T(8,128)(2,1)S(1)}, bf16[112,768]{1,0:T(8,128)(2,1)S(1)}, u32[]{:S(2)}, u32[]{:S(2)}) collective-permute-start(bf16[112,768]{1,0:T(8,128)(2,1)S(1)} %copy-done.30), channel_id=1, source_target_pairs={{0,3},{1,0},{2,1},{3,2},{4,7},{5,4},{6,5},{7,6},{8,11},{9,8},{10,9... | collective-permute-start | bytes 516104 | tf_op jit(solution)/shard_map/ppermute | solution.py:311
  80.7 2.0 %collective-permute-done.10.a1 = bf16[112,768]{1,0:T(8,128)(2,1)S(1)} collective-permute-done((bf16[112,768]{1,0:T(8,128)(2,1)S(1)}, bf16[112,768]{1,0:T(8,128)(2,1)S(1)}, u32[]{:S(2)}, u32[]{:S(2)}) %collective-permute-start.10) | collective-permute-done | bytes 172064 | tf_op jit(solution)/shard_map/ppermute | solution.py:311
  82.7 3.7 %collective-permute-done.11.a2 = bf16[112,768]{1,0:T(8,128)(2,1)S(1)} collective-permute-done((bf16[112,768]{1,0:T(8,128)(2,1)S(1)}, bf16[112,768]{1,0:T(8,128)(2,1)S(1)}, u32[]{:S(2)}, u32[]{:S(2)}) %collective-permute-start.11) | collective-permute-done | bytes 172064 | tf_op jit(solution)/shard_map/ppermute | solution.py:311
  86.8 1.7 collective-permute-start.13
  88.5 2.4 %collective-permute-start.14 = (f32[8,128]{1,0:T(8,128)S(1)}, f32[8,128]{1,0:T(8,128)S(1)}, u32[]{:S(2)}, u32[]{:S(2)}) collective-permute-start(f32[8,128]{1,0:T(8,128)S(1)} %add.65), channel_id=1, source_target_pairs={{0,2},{1,3},{2,0},{3,1},{4,6},{5,7},{6,4},{7,5},{8,10},{9,11},{10,... | collective-permute-start | bytes 12296 | tf_op jit(solution)/shard_map/ppermute | solution.py:311
  94.5 2.0 %collective-permute-start.16 = (f32[8,128]{1,0:T(8,128)S(1)}, f32[8,128]{1,0:T(8,128)S(1)}, u32[]{:S(2)}, u32[]{:S(2)}) collective-permute-start(f32[8,128]{1,0:T(8,128)S(1)} %add_add_fusion), channel_id=1, source_target_pairs={{0,8},{4,12},{8,16},{12,20},{16,24},{20,28},{24,32},{28,36},{32,40... | collective-permute-start | bytes 12296 | tf_op jit(solution)/shard_map/ppermute | solution.py:308
  98.2 3.3 %collective-permute-start.18 = (f32[3,8,128]{2,1,0:T(8,128)S(1)}, f32[3,8,128]{2,1,0:T(8,128)S(1)}, u32[]{:S(2)}, u32[]{:S(2)}) collective-permute-start(f32[3,8,128]{2,1,0:T(8,128)S(1)} %pad_maximum_fusion.2), channel_id=1, source_target_pairs={{0,16},{4,20},{8,24},{12,28},{16,32},{20,36},{24,40},{28,44},{32,4... | collective-permute-start | bytes 36872 | tf_op jit(solution)/shard_map/ppermute | solution.py:308
  101.5 2.9 %collective-permute-start.19 = (f32[3,8,128]{2,1,0:T(8,128)S(1)}, f32[3,8,128]{2,1,0:T(8,128)S(1)}, u32[]{:S(2)}, u32[]{:S(2)}) collective-permute-start(f32[3,8,128]{2,1,0:T(8,128)S(1)} %pad_maximum_fusion.2), channel_id=1, source_target_pairs={{0,240},{4,244},{8,248},{12,252},{16,0},{20,4},{24,8},{28,12},{32,... | collective-permute-start | bytes 36872 | tf_op jit(solution)/shard_map/ppermute | solution.py:308
  109.8 16.2 %weight.1 = (f32[3,48,896]{2,1,0:T(8,128)}, bf16[3,48,896]{2,1,0:T(8,128)(2,1)}, bf16[3,48,896]{2,1,0:T(8,128)(2,1)}, bf16[3,48,896]{2,1,0:T(8,128)(2,1)}) custom-call(s32[4]{0:T(128)} %pad_add_fusion.at_ref, f32[24]{0:T(128)} %mul.48.keep_ref, f32[8]{0:T(128)} %copy-done.28, f32[1]{0:T(128)} %bitcast.11.loss_ref, bf16[112,768]{1,0:T(8,128)(2,1)} %get-tuple-element.62.a0, ...), custom_call_target="tpu_custom_call" | custom-call | tf_op jit(solution)/shard_map/weight/pallas_call | solution.py:418
  127.4 2.9 %collective-permute-start.26 = (bf16[3,48,896]{2,1,0:T(8,128)(2,1)}, bf16[3,48,896]{2,1,0:T(8,128)(2,1)S(1)}, u32[]{:S(2)}, u32[]{:S(2)}) collective-permute-start(bf16[3,48,896]{2,1,0:T(8,128)(2,1)} %get-tuple-element.75), channel_id=1, source_target_pairs={{0,128},{4,132},{8,136},{12,140},{16,144},{20,148},{24,152},{28,15... | collective-permute-start | bytes 774152 | tf_op jit(solution)/shard_map/ppermute | solution.py:314
  131.6 4.3 %collective-permute-done.25.refs_1_ = bf16[3,48,896]{2,1,0:T(8,128)(2,1)S(1)} collective-permute-done((bf16[3,48,896]{2,1,0:T(8,128)(2,1)}, bf16[3,48,896]{2,1,0:T(8,128)(2,1)S(1)}, u32[]{:S(2)}, u32[]{:S(2)}) %collective-permute-start.25) | collective-permute-done | bytes 258080 | tf_op jit(solution)/shard_map/ppermute | solution.py:314
  135.9 6.7 %collective-permute-done.26.refs_2_ = bf16[3,48,896]{2,1,0:T(8,128)(2,1)S(1)} collective-permute-done((bf16[3,48,896]{2,1,0:T(8,128)(2,1)}, bf16[3,48,896]{2,1,0:T(8,128)(2,1)S(1)}, u32[]{:S(2)}, u32[]{:S(2)}) %collective-permute-start.26) | collective-permute-done | bytes 258080 | tf_op jit(solution)/shard_map/ppermute | solution.py:314
  143.4 2.4 %add.93 = (f32[24,896]{1,0:T(8,128)}, bf16[24,896]{1,0:T(8,128)(2,1)}, bf16[24,896]{1,0:T(8,128)(2,1)}, bf16[24,896]{1,0:T(8,128)(2,1)}, bf16[24,896]{1,0:T(8,12...) custom-call(s32[4]{0:T(128)} %pad_add_fusion.at_ref, ...), custom_call_target="tpu_custom_call" | custom-call | tf_op jit(solution)/shard_map/add/pallas_call | solution.py:435
  145.8 4.5 %collective-permute-start.28 = (bf16[24,896]{1,0:T(8,128)(2,1)}, bf16[24,896]{1,0:T(8,128)(2,1)S(1)}, u32[]{:S(2)}, u32[]{:S(2)}) collective-permute-start(bf16[24,896]{1,0:T(8,128)(2,1)} %get-tuple-element.78), channel_id=1, source_target_pairs={{0,8},{4,12},{8,16},{12,20},{16,24},{20,28},{24,32},{28,36},{32,40... | collective-permute-start | bytes 129032 | tf_op jit(solution)/shard_map/ppermute | solution.py:317
  150.3 4.2 %collective-permute-start.30 = (bf16[24,896]{1,0:T(8,128)(2,1)}, bf16[24,896]{1,0:T(8,128)(2,1)S(1)}, u32[]{:S(2)}, u32[]{:S(2)}) collective-permute-start(bf16[24,896]{1,0:T(8,128)(2,1)} %get-tuple-element.80), channel_id=1, source_target_pairs={{0,24},{4,28},{8,32},{12,36},{16,40},{20,44},{24,48},{28,52},{32,5... | collective-permute-start | bytes 129032 | tf_op jit(solution)/shard_map/ppermute | solution.py:317
  154.4 1.9 %collective-permute-start.31 = (bf16[24,896]{1,0:T(8,128)(2,1)}, bf16[24,896]{1,0:T(8,128)(2,1)S(1)}, u32[]{:S(2)}, u32[]{:S(2)}) collective-permute-start(bf16[24,896]{1,0:T(8,128)(2,1)} %get-tuple-element.81), channel_id=1, source_target_pairs={{0,32},{4,36},{8,40},{12,44},{16,48},{20,52},{24,56},{28,60},{32,0... | collective-permute-start | bytes 129032 | tf_op jit(solution)/shard_map/ppermute | solution.py:317
  156.3 3.1 %collective-permute-start.32 = (bf16[24,896]{1,0:T(8,128)(2,1)}, bf16[24,896]{1,0:T(8,128)(2,1)S(1)}, u32[]{:S(2)}, u32[]{:S(2)}) collective-permute-start(bf16[24,896]{1,0:T(8,128)(2,1)} %get-tuple-element.82), channel_id=1, source_target_pairs={{0,40},{4,44},{8,48},{12,52},{16,56},{20,60},{24,0},{28,4},{32,8},... | collective-permute-start | bytes 129032 | tf_op jit(solution)/shard_map/ppermute | solution.py:317
  159.4 2.9 %collective-permute-start.33 = (bf16[24,896]{1,0:T(8,128)(2,1)}, bf16[24,896]{1,0:T(8,128)(2,1)S(1)}, u32[]{:S(2)}, u32[]{:S(2)}) collective-permute-start(bf16[24,896]{1,0:T(8,128)(2,1)} %get-tuple-element.83), channel_id=1, source_target_pairs={{0,48},{4,52},{8,56},{12,60},{16,0},{20,4},{24,8},{28,12},{32,16},... | collective-permute-start | bytes 129032 | tf_op jit(solution)/shard_map/ppermute | solution.py:317
  162.3 1.7 collective-permute-done.31.refs_4_
  (135 shorter events, 33.7 us)
Async XLA Ops:
  7.2 59.8 %all-gather.2.cloned.1.call-start = ((), (), s32[]{:S(2)}) async-start(), calls=%async_computation | async-start | bytes 2949120 | tf_op jit(solution)/shard_map/all_gather | solution.py:335
  9.8 14.3 %collective-permute-start = (bf16[2,192,384]{2,1,0:T(8,128)(2,1)}, bf16[2,192,384]{2,1,0:T(8,128)(2,1)S(1)}, u32[]{:S(2)}, u32[]{:S(2)}) collective-permute-start(bf16[2,192,384]{2,1,0:T(8,128)(2,1)} %get-tuple-element.46), channel_id=1, source_target_pairs={{0,4},{4,8},{8,12},{12,16},{16,20},{20,24},{24,28},{28,32},{32,36}... | collective-permute-start | bytes 884744 | tf_op jit(solution)/shard_map/ppermute | solution.py:348
  11.7 12.4 %collective-permute-start.1 = (bf16[1,192,384]{2,1,0:T(8,128)(2,1)}, bf16[1,192,384]{2,1,0:T(8,128)(2,1)S(1)}, u32[]{:S(2)}, u32[]{:S(2)}) collective-permute-start(bf16[1,192,384]{2,1,0:T(8,128)(2,1)} %get-tuple-element.47), channel_id=1, source_target_pairs={{4,12},{12,20},{20,28},{28,36},{36,44},{44,52},{52,60},{60,68},{68... | collective-permute-start | bytes 442376 | tf_op jit(solution)/shard_map/ppermute | solution.py:353
  12.4 20.0 %collective-permute-start.4 = (bf16[2,24,384]{2,1,0:T(8,128)(2,1)}, bf16[2,24,384]{2,1,0:T(8,128)(2,1)S(1)}, u32[]{:S(2)}, u32[]{:S(2)}) collective-permute-start(bf16[2,24,384]{2,1,0:T(8,128)(2,1)} %get-tuple-element.51), channel_id=1, source_target_pairs={{0,5},{1,6},{2,7},{4,9},{5,10},{6,11},{8,13},{9,14},{10,15},{12,17... | collective-permute-start | bytes 110600 | tf_op jit(solution)/shard_map/ppermute | solution.py:350
  20.3 14.2 %collective-permute-start.5 = (bf16[2,24,384]{2,1,0:T(8,128)(2,1)}, bf16[2,24,384]{2,1,0:T(8,128)(2,1)S(1)}, u32[]{:S(2)}, u32[]{:S(2)}) collective-permute-start(bf16[2,24,384]{2,1,0:T(8,128)(2,1)} %get-tuple-element.52), channel_id=1, source_target_pairs={{1,4},{2,5},{3,6},{5,8},{6,9},{7,10},{9,12},{10,13},{11,14},{13,16... | collective-permute-start | bytes 110600 | tf_op jit(solution)/shard_map/ppermute | solution.py:351
  24.2 42.7 %collective-permute-start.6 = (bf16[1,192,384]{2,1,0:T(8,128)(2,1)S(1)}, bf16[1,192,384]{2,1,0:T(8,128)(2,1)S(1)}, u32[]{:S(2)}, u32[]{:S(2)}) collective-permute-start(bf16[1,192,384]{2,1,0:T(8,128)(2,1)S(1)} %slice_select_fusion.p0), channel_id=1, source_target_pairs={{0,1},{1,2},{2,3},{3,0},{4,5},{5,6},{6,7},{7,4},{8,9},{9,10},{10,1... | collective-permute-start | bytes 442376 | tf_op jit(solution)/shard_map/ppermute | solution.py:311
  26.4 40.5 %collective-permute-start.7 = (bf16[1,192,384]{2,1,0:T(8,128)(2,1)S(1)}, bf16[1,192,384]{2,1,0:T(8,128)(2,1)S(1)}, u32[]{:S(2)}, u32[]{:S(2)}) collective-permute-start(bf16[1,192,384]{2,1,0:T(8,128)(2,1)S(1)} %slice_select_fusion.p0), channel_id=1, source_target_pairs={{0,2},{1,3},{2,0},{3,1},{4,6},{5,7},{6,4},{7,5},{8,10},{9,11},{10,... | collective-permute-start | bytes 442376 | tf_op jit(solution)/shard_map/ppermute | solution.py:311
  28.5 38.5 %collective-permute-start.8 = (bf16[1,192,384]{2,1,0:T(8,128)(2,1)S(1)}, bf16[1,192,384]{2,1,0:T(8,128)(2,1)S(1)}, u32[]{:S(2)}, u32[]{:S(2)}) collective-permute-start(bf16[1,192,384]{2,1,0:T(8,128)(2,1)S(1)} %slice_select_fusion.p0), channel_id=1, source_target_pairs={{0,3},{1,0},{2,1},{3,2},{4,7},{5,4},{6,5},{7,6},{8,11},{9,8},{10,9... | collective-permute-start | bytes 442376 | tf_op jit(solution)/shard_map/ppermute | solution.py:311
  32.4 10.2 %collective-permute-start.2 = (bf16[4,24,384]{2,1,0:T(8,128)(2,1)}, bf16[4,24,384]{2,1,0:T(8,128)(2,1)S(1)}, u32[]{:S(2)}, u32[]{:S(2)}) collective-permute-start(bf16[4,24,384]{2,1,0:T(8,128)(2,1)} %get-tuple-element.49), channel_id=1, source_target_pairs={{0,1},{1,2},{2,3},{4,5},{5,6},{6,7},{8,9},{9,10},{10,11},{12,13},{... | collective-permute-start | bytes 221192 | tf_op jit(solution)/shard_map/ppermute | solution.py:345
  34.6 10.3 %collective-permute-start.3 = (bf16[4,24,384]{2,1,0:T(8,128)(2,1)}, bf16[4,24,384]{2,1,0:T(8,128)(2,1)S(1)}, u32[]{:S(2)}, u32[]{:S(2)}) collective-permute-start(bf16[4,24,384]{2,1,0:T(8,128)(2,1)} %get-tuple-element.50), channel_id=1, source_target_pairs={{1,0},{2,1},{3,2},{5,4},{6,5},{7,6},{9,8},{10,9},{11,10},{13,12},{... | collective-permute-start | bytes 221192 | tf_op jit(solution)/shard_map/ppermute | solution.py:346
  62.4 3.8 %collective-permute-start.9 = (f32[8,128]{1,0:T(8,128)}, f32[8,128]{1,0:T(8,128)S(1)}, u32[]{:S(2)}, u32[]{:S(2)}) collective-permute-start(f32[8,128]{1,0:T(8,128)} %get-tuple-element.55), channel_id=1, source_target_pairs={{0,4},{4,0},{8,12},{12,8},{16,20},{20,16},{24,28},{28,24},{32,36},... | collective-permute-start | bytes 12296 | tf_op jit(solution)/shard_map/ppermute | solution.py:305
  74.5 33.9 %collective-permute-start.24 = (bf16[5,768,256]{2,1,0:T(8,128)(2,1)}, bf16[5,768,256]{2,1,0:T(8,128)(2,1)S(1)}, u32[]{:S(2)}, u32[]{:S(2)}) collective-permute-start(bf16[5,768,256]{2,1,0:T(8,128)(2,1)} %get-tuple-element.72), channel_id=1, source_target_pairs={{0,4},{4,0},{8,12},{12,8},{16,20},{20,16},{24,28},{28,24},{32,36},... | collective-permute-start | bytes 5898248 | tf_op jit(solution)/shard_map/ppermute | solution.py:305
  74.8 7.9 %collective-permute-start.10 = (bf16[112,768]{1,0:T(8,128)(2,1)S(1)}, bf16[112,768]{1,0:T(8,128)(2,1)S(1)}, u32[]{:S(2)}, u32[]{:S(2)}) collective-permute-start(bf16[112,768]{1,0:T(8,128)(2,1)S(1)} %copy-done.32), channel_id=1, source_target_pairs={{0,1},{1,2},{2,3},{3,0},{4,5},{5,6},{6,7},{7,4},{8,9},{9,10},{10,1... | collective-permute-start | bytes 516104 | tf_op jit(solution)/shard_map/ppermute | solution.py:311
  74.8 11.6 %collective-permute-start.11 = (bf16[112,768]{1,0:T(8,128)(2,1)S(1)}, bf16[112,768]{1,0:T(8,128)(2,1)S(1)}, u32[]{:S(2)}, u32[]{:S(2)}) collective-permute-start(bf16[112,768]{1,0:T(8,128)(2,1)S(1)} %copy-done.31), channel_id=1, source_target_pairs={{0,2},{1,3},{2,0},{3,1},{4,6},{5,7},{6,4},{7,5},{8,10},{9,11},{10,... | collective-permute-start | bytes 516104 | tf_op jit(solution)/shard_map/ppermute | solution.py:311
  78.1 8.6 %collective-permute-start.12 = (bf16[112,768]{1,0:T(8,128)(2,1)S(1)}, bf16[112,768]{1,0:T(8,128)(2,1)S(1)}, u32[]{:S(2)}, u32[]{:S(2)}) collective-permute-start(bf16[112,768]{1,0:T(8,128)(2,1)S(1)} %copy-done.30), channel_id=1, source_target_pairs={{0,3},{1,0},{2,1},{3,2},{4,7},{5,4},{6,5},{7,6},{8,11},{9,8},{10,9... | collective-permute-start | bytes 516104 | tf_op jit(solution)/shard_map/ppermute | solution.py:311
  86.8 5.9 %collective-permute-start.13 = (f32[8,128]{1,0:T(8,128)S(1)}, f32[8,128]{1,0:T(8,128)S(1)}, u32[]{:S(2)}, u32[]{:S(2)}) collective-permute-start(f32[8,128]{1,0:T(8,128)S(1)} %add.65), channel_id=1, source_target_pairs={{0,1},{1,2},{2,3},{3,0},{4,5},{5,6},{6,7},{7,4},{8,9},{9,10},{10,1... | collective-permute-start | bytes 12296 | tf_op jit(solution)/shard_map/ppermute | solution.py:311
  88.5 5.1 %collective-permute-start.14 = (f32[8,128]{1,0:T(8,128)S(1)}, f32[8,128]{1,0:T(8,128)S(1)}, u32[]{:S(2)}, u32[]{:S(2)}) collective-permute-start(f32[8,128]{1,0:T(8,128)S(1)} %add.65), channel_id=1, source_target_pairs={{0,2},{1,3},{2,0},{3,1},{4,6},{5,7},{6,4},{7,5},{8,10},{9,11},{10,... | collective-permute-start | bytes 12296 | tf_op jit(solution)/shard_map/ppermute | solution.py:311
  94.5 3.7 %collective-permute-start.16 = (f32[8,128]{1,0:T(8,128)S(1)}, f32[8,128]{1,0:T(8,128)S(1)}, u32[]{:S(2)}, u32[]{:S(2)}) collective-permute-start(f32[8,128]{1,0:T(8,128)S(1)} %add_add_fusion), channel_id=1, source_target_pairs={{0,8},{4,12},{8,16},{12,20},{16,24},{20,28},{24,32},{28,36},{32,40... | collective-permute-start | bytes 12296 | tf_op jit(solution)/shard_map/ppermute | solution.py:308
  98.2 7.9 %collective-permute-start.18 = (f32[3,8,128]{2,1,0:T(8,128)S(1)}, f32[3,8,128]{2,1,0:T(8,128)S(1)}, u32[]{:S(2)}, u32[]{:S(2)}) collective-permute-start(f32[3,8,128]{2,1,0:T(8,128)S(1)} %pad_maximum_fusion.2), channel_id=1, source_target_pairs={{0,16},{4,20},{8,24},{12,28},{16,32},{20,36},{24,40},{28,44},{32,4... | collective-permute-start | bytes 36872 | tf_op jit(solution)/shard_map/ppermute | solution.py:308
  101.5 4.6 %collective-permute-start.19 = (f32[3,8,128]{2,1,0:T(8,128)S(1)}, f32[3,8,128]{2,1,0:T(8,128)S(1)}, u32[]{:S(2)}, u32[]{:S(2)}) collective-permute-start(f32[3,8,128]{2,1,0:T(8,128)S(1)} %pad_maximum_fusion.2), channel_id=1, source_target_pairs={{0,240},{4,244},{8,248},{12,252},{16,0},{20,4},{24,8},{28,12},{32,... | collective-permute-start | bytes 36872 | tf_op jit(solution)/shard_map/ppermute | solution.py:308
  104.4 3.8 %collective-permute-start.20 = (bf16[112,768]{1,0:T(8,128)(2,1)S(1)}, bf16[112,768]{1,0:T(8,128)(2,1)S(1)}, u32[]{:S(2)}, u32[]{:S(2)}) collective-permute-start(bf16[112,768]{1,0:T(8,128)(2,1)S(1)} %copy-done.6), channel_id=1, source_target_pairs={{0,4},{4,0},{8,12},{12,8},{16,20},{20,16},{24,28},{28,24},{32,36},... | collective-permute-start | bytes 516104 | tf_op jit(solution)/shard_map/ppermute | solution.py:305
  104.4 3.8 %collective-permute-start.21 = (bf16[112,768]{1,0:T(8,128)(2,1)S(1)}, bf16[112,768]{1,0:T(8,128)(2,1)S(1)}, u32[]{:S(2)}, u32[]{:S(2)}) collective-permute-start(bf16[112,768]{1,0:T(8,128)(2,1)S(1)} %collective-permute-done.10.a1), channel_id=1, source_target_pairs={{0,4},{4,0},{8,12},{12,8},{16,20},{20,16},{24,28},{28,24},{32,36},... | collective-permute-start | bytes 516104 | tf_op jit(solution)/shard_map/ppermute | solution.py:305
  126.0 9.9 %collective-permute-start.25 = (bf16[3,48,896]{2,1,0:T(8,128)(2,1)}, bf16[3,48,896]{2,1,0:T(8,128)(2,1)S(1)}, u32[]{:S(2)}, u32[]{:S(2)}) collective-permute-start(bf16[3,48,896]{2,1,0:T(8,128)(2,1)} %get-tuple-element.74), channel_id=1, source_target_pairs={{0,64},{4,68},{8,72},{12,76},{16,80},{20,84},{24,88},{28,92},{32,9... | collective-permute-start | bytes 774152 | tf_op jit(solution)/shard_map/ppermute | solution.py:314
  127.4 15.2 %collective-permute-start.26 = (bf16[3,48,896]{2,1,0:T(8,128)(2,1)}, bf16[3,48,896]{2,1,0:T(8,128)(2,1)S(1)}, u32[]{:S(2)}, u32[]{:S(2)}) collective-permute-start(bf16[3,48,896]{2,1,0:T(8,128)(2,1)} %get-tuple-element.75), channel_id=1, source_target_pairs={{0,128},{4,132},{8,136},{12,140},{16,144},{20,148},{24,152},{28,15... | collective-permute-start | bytes 774152 | tf_op jit(solution)/shard_map/ppermute | solution.py:314
  130.3 12.3 %collective-permute-start.27 = (bf16[3,48,896]{2,1,0:T(8,128)(2,1)}, bf16[3,48,896]{2,1,0:T(8,128)(2,1)S(1)}, u32[]{:S(2)}, u32[]{:S(2)}) collective-permute-start(bf16[3,48,896]{2,1,0:T(8,128)(2,1)} %get-tuple-element.76), channel_id=1, source_target_pairs={{0,192},{4,196},{8,200},{12,204},{16,208},{20,212},{24,216},{28,22... | collective-permute-start | bytes 774152 | tf_op jit(solution)/shard_map/ppermute | solution.py:314
  145.8 13.6 %collective-permute-start.28 = (bf16[24,896]{1,0:T(8,128)(2,1)}, bf16[24,896]{1,0:T(8,128)(2,1)S(1)}, u32[]{:S(2)}, u32[]{:S(2)}) collective-permute-start(bf16[24,896]{1,0:T(8,128)(2,1)} %get-tuple-element.78), channel_id=1, source_target_pairs={{0,8},{4,12},{8,16},{12,20},{16,24},{20,28},{24,32},{28,36},{32,40... | collective-permute-start | bytes 129032 | tf_op jit(solution)/shard_map/ppermute | solution.py:317
  150.3 12.0 %collective-permute-start.29 = (bf16[24,896]{1,0:T(8,128)(2,1)}, bf16[24,896]{1,0:T(8,128)(2,1)S(1)}, u32[]{:S(2)}, u32[]{:S(2)}) collective-permute-start(bf16[24,896]{1,0:T(8,128)(2,1)} %get-tuple-element.79), channel_id=1, source_target_pairs={{0,16},{4,20},{8,24},{12,28},{16,32},{20,36},{24,40},{28,44},{32,4... | collective-permute-start | bytes 129032 | tf_op jit(solution)/shard_map/ppermute | solution.py:317
  150.3 12.1 %collective-permute-start.30 = (bf16[24,896]{1,0:T(8,128)(2,1)}, bf16[24,896]{1,0:T(8,128)(2,1)S(1)}, u32[]{:S(2)}, u32[]{:S(2)}) collective-permute-start(bf16[24,896]{1,0:T(8,128)(2,1)} %get-tuple-element.80), channel_id=1, source_target_pairs={{0,24},{4,28},{8,32},{12,36},{16,40},{20,44},{24,48},{28,52},{32,5... | collective-permute-start | bytes 129032 | tf_op jit(solution)/shard_map/ppermute | solution.py:317
  154.4 9.7 %collective-permute-start.31 = (bf16[24,896]{1,0:T(8,128)(2,1)}, bf16[24,896]{1,0:T(8,128)(2,1)S(1)}, u32[]{:S(2)}, u32[]{:S(2)}) collective-permute-start(bf16[24,896]{1,0:T(8,128)(2,1)} %get-tuple-element.81), channel_id=1, source_target_pairs={{0,32},{4,36},{8,40},{12,44},{16,48},{20,52},{24,56},{28,60},{32,0... | collective-permute-start | bytes 129032 | tf_op jit(solution)/shard_map/ppermute | solution.py:317
  156.3 9.0 %collective-permute-start.32 = (bf16[24,896]{1,0:T(8,128)(2,1)}, bf16[24,896]{1,0:T(8,128)(2,1)S(1)}, u32[]{:S(2)}, u32[]{:S(2)}) collective-permute-start(bf16[24,896]{1,0:T(8,128)(2,1)} %get-tuple-element.82), channel_id=1, source_target_pairs={{0,40},{4,44},{8,48},{12,52},{16,56},{20,60},{24,0},{28,4},{32,8},... | collective-permute-start | bytes 129032 | tf_op jit(solution)/shard_map/ppermute | solution.py:317
  159.4 7.3 %collective-permute-start.33 = (bf16[24,896]{1,0:T(8,128)(2,1)}, bf16[24,896]{1,0:T(8,128)(2,1)S(1)}, u32[]{:S(2)}, u32[]{:S(2)}) collective-permute-start(bf16[24,896]{1,0:T(8,128)(2,1)} %get-tuple-element.83), channel_id=1, source_target_pairs={{0,48},{4,52},{8,56},{12,60},{16,0},{20,4},{24,8},{28,12},{32,16},... | collective-permute-start | bytes 129032 | tf_op jit(solution)/shard_map/ppermute | solution.py:317
  162.3 4.5 %collective-permute-start.34 = (bf16[24,896]{1,0:T(8,128)(2,1)}, bf16[24,896]{1,0:T(8,128)(2,1)S(1)}, u32[]{:S(2)}, u32[]{:S(2)}) collective-permute-start(bf16[24,896]{1,0:T(8,128)(2,1)} %get-tuple-element.84), channel_id=1, source_target_pairs={{0,56},{4,60},{8,0},{12,4},{16,8},{20,12},{24,16},{28,20},{32,24},... | collective-permute-start | bytes 129032 | tf_op jit(solution)/shard_map/ppermute | solution.py:317
  (37 other events, 330.7 us)
Sparse Core Ops, SparseCore 0:
  9.8 45.1 all-gather.1
